TPU v7x, 512 devices: a whole 4x4x16 slice. The times are simulated.
512 devices in a mesh: frames: 8 (over y, core), tiles: 64 (over z, x).
Axes of the slice: x: 4, y: 4, z: 16, core: 2. Of those that a mesh axis runs over, the one named last changes fastest.
Arguments:
- inputs: bfloat16 [8, 64, 128, 1024], P('frames', 'tiles'), may hold values from -0.375 to 0.375
- grad_out: bfloat16 [8, 64, 128, 1024], P('frames', 'tiles'), may hold values from -0.375 to 0.375
- b_proj: bfloat16 [8, 64, 128, 128], P('frames', 'tiles'), may hold values from -0.5 to 0.5
- c_proj: bfloat16 [8, 64, 128, 128], P('frames', 'tiles'), may hold values from -0.5 to 0.5
- log_decay: bfloat16 [16, 8, 64, 128], P(None, 'frames', 'tiles'), may hold values from -0.6 to 0
- saved_raster: float32 [8, 64, 16, 64, 128], P('frames', 'tiles'), may hold values from -6 to 6
- saved_column: float32 [8, 64, 16, 64, 128], P('frames', 'tiles'), may hold values from -6 to 6
Outputs:
- grad_x: bfloat16 [8, 64, 128, 1024], P('frames', 'tiles')
- grad_b: bfloat16 [8, 64, 128, 128], P('frames', 'tiles')
- grad_c: bfloat16 [8, 64, 128, 128], P('frames', 'tiles')
All inputs are finite; a program needn't handle non-finite values.
Results may differ from a plain program's by a relative error of at most 0.015.
Values may be sent and summed in bfloat16 or wider, within the bound.
A program may use at most 64 MiB of HBM per device.

v0:
```python
import jax
import jax.numpy as jnp
from jax import lax
from jax.sharding import PartitionSpec as P

HEADS = 16
HEAD_DIM = 64
STATE = 128


def shifted(x, axis, by):
    devices = lax.axis_size(axis)
    pairs = [(i, i + by) for i in range(devices) if 0 <= i + by < devices]
    return lax.ppermute(x, axis, pairs)


def block_element(grad_rows, c_rows, decay_rows):
    length = grad_rows.shape[0]
    cumulative = jnp.cumsum(decay_rows.astype(jnp.float32), axis=0)
    weighted = (jnp.exp(cumulative)[:, :, None] * c_rows.astype(jnp.float32)[:, None, :]).astype(
        jnp.bfloat16
    )
    grad_heads = grad_rows.reshape(length, HEADS, HEAD_DIM)
    state_term = jnp.einsum(
        "tho,thn->hon", grad_heads, weighted, preferred_element_type=jnp.float32
    )
    return (cumulative, jnp.exp(cumulative[-1]), state_term)


def block_grads(x_rows, grad_rows, b_rows, c_rows, cumulative, saved, carried):
    length = x_rows.shape[0]
    block_total = cumulative[-1]
    input_heads = x_rows.reshape(length, HEADS, HEAD_DIM)
    grad_heads = grad_rows.reshape(length, HEADS, HEAD_DIM)
    row_index = lax.broadcasted_iota(jnp.int32, (length, length), 0)
    col_index = lax.broadcasted_iota(jnp.int32, (length, length), 1)
    causal = row_index >= col_index
    cum_heads = cumulative.T
    log_gap = cum_heads[:, :, None] - cum_heads[:, None, :]
    weight = jnp.where(causal[None], jnp.exp(jnp.minimum(log_gap, 0.0)), 0.0)
    scores = jnp.einsum("tho,sho->hts", grad_heads, input_heads, preferred_element_type=jnp.float32)
    mixed_r = (weight * scores).astype(jnp.bfloat16)
    pairing = jnp.dot(c_rows, b_rows.T, preferred_element_type=jnp.float32)
    mixed_z = (weight * pairing[None]).astype(jnp.bfloat16)
    carry_low = carried.astype(jnp.bfloat16)
    saved_low = saved.astype(jnp.bfloat16)
    tail_scale = jnp.exp(block_total[None, :] - cumulative)
    head_scale = jnp.exp(cumulative)
    grad_input = jnp.einsum("hst,sho->tho", mixed_z, grad_heads, preferred_element_type=jnp.float32)
    grad_input = grad_input + tail_scale[:, :, None] * jnp.einsum(
        "tn,hon->tho", b_rows, carry_low, preferred_element_type=jnp.float32
    )
    grad_bmap = jnp.einsum("hst,sn->tn", mixed_r, c_rows, preferred_element_type=jnp.float32)
    grad_bmap = grad_bmap + jnp.sum(
        tail_scale[:, :, None]
        * jnp.einsum("tho,hon->thn", input_heads, carry_low, preferred_element_type=jnp.float32),
        axis=1,
    )
    grad_cmap = jnp.einsum("hts,sn->tn", mixed_r, b_rows, preferred_element_type=jnp.float32)
    grad_cmap = grad_cmap + jnp.sum(
        head_scale[:, :, None]
        * jnp.einsum("tho,hon->thn", grad_heads, saved_low, preferred_element_type=jnp.float32),
        axis=1,
    )
    return (grad_input.reshape(length, HEADS * HEAD_DIM), grad_bmap, grad_cmap)


def shards(inputs, grad_out, b_proj, c_proj, log_decay, saved_raster, saved_column):
    frames_here, row_count, width_cells, channels = inputs.shape
    length = frames_here * row_count * width_cells
    decay_last = jnp.transpose(log_decay, (1, 2, 3, 0))

    def flatten(array):
        return array.reshape(length, array.shape[-1])

    row_cum, horizontal_entire, row_term = block_element(
        flatten(grad_out), flatten(c_proj), flatten(decay_last)
    )
    exchanged = (
        lax.all_to_all(inputs, "tiles", split_axis=2, concat_axis=1, tiled=True),
        lax.all_to_all(grad_out, "tiles", split_axis=2, concat_axis=1, tiled=True),
        lax.all_to_all(b_proj, "tiles", split_axis=2, concat_axis=1, tiled=True),
        lax.all_to_all(c_proj, "tiles", split_axis=2, concat_axis=1, tiled=True),
        lax.all_to_all(decay_last, "tiles", split_axis=2, concat_axis=1, tiled=True),
    )
    frame_height = exchanged[0].shape[1]
    columns = exchanged[0].shape[2]

    def by_column(array):
        return jnp.transpose(array, (0, 2, 1, 3)).reshape(length, array.shape[-1])

    col_inputs, col_grad, col_bmap, col_cmap, col_decay = [by_column(array) for array in exchanged]
    col_cum, col_all, column_term = block_element(col_grad, col_cmap, col_decay)
    row_carry = jnp.zeros((HEADS, HEAD_DIM, STATE), jnp.float32)
    col_carry = jnp.zeros((HEADS, HEAD_DIM, STATE), jnp.float32)
    for section in range(lax.axis_size("frames") - 1):
        leaving_state = (
            horizontal_entire[:, None, None] * row_carry + row_term,
            col_all[:, None, None] * col_carry + column_term,
        )
        row_carry, col_carry = (
            shifted(leaving_state[0].astype(jnp.bfloat16), "frames", -1).astype(jnp.float32),
            shifted(leaving_state[1].astype(jnp.bfloat16), "frames", -1).astype(jnp.float32),
        )
    row_grad_x, row_grad_b, row_gradient_c = block_grads(
        flatten(inputs),
        flatten(grad_out),
        flatten(b_proj),
        flatten(c_proj),
        row_cum,
        saved_raster.reshape(HEADS, HEAD_DIM, STATE),
        row_carry,
    )
    col_grad_x, col_grad_b, col_grad_c = block_grads(
        col_inputs,
        col_grad,
        col_bmap,
        col_cmap,
        col_cum,
        saved_column.reshape(HEADS, HEAD_DIM, STATE),
        col_carry,
    )

    def to_columns(array):
        return jnp.transpose(
            array.astype(jnp.bfloat16).reshape(frames_here, columns, frame_height, array.shape[-1]),
            (0, 2, 1, 3),
        )

    returned = (
        lax.all_to_all(to_columns(col_grad_x), "tiles", split_axis=1, concat_axis=2, tiled=True),
        lax.all_to_all(to_columns(col_grad_b), "tiles", split_axis=1, concat_axis=2, tiled=True),
        lax.all_to_all(to_columns(col_grad_c), "tiles", split_axis=1, concat_axis=2, tiled=True),
    )

    def finish(row_part, col_part):
        return (
            row_part.reshape(frames_here, row_count, width_cells, row_part.shape[-1])
            + col_part.astype(jnp.float32)
        ).astype(jnp.bfloat16)

    return (
        finish(row_grad_x, returned[0]),
        finish(row_grad_b, returned[1]),
        finish(row_gradient_c, returned[2]),
    )


def solution(mesh):
    in_specs = (
        P("frames", "tiles", None, None),
        P("frames", "tiles", None, None),
        P("frames", "tiles", None, None),
        P("frames", "tiles", None, None),
        P(None, "frames", "tiles", None),
        P("frames", "tiles", None, None, None),
        P("frames", "tiles", None, None, None),
    )
    out_specs = (
        P("frames", "tiles", None, None),
        P("frames", "tiles", None, None),
        P("frames", "tiles", None, None),
    )
    return jax.shard_map(shards, mesh=mesh, in_specs=in_specs, out_specs=out_specs, check_vma=False)
```

profile of v0, /device:TPU:1, one launch (start us, length us, event | category | flops | bytes accessed | tf_op | source)
XLA Modules:
  0.0 246.6 jit_solution(9619099634372276854)
XLA Ops:
  0.6 1.4 copy.149
  2.1 19.1 %all-to-all-start = ((bf16[1,1,128,16]{3,1,0,2:T(2,128)(2,1)}), bf16[1,1,128,16]{3,1,0,2:T(2,128)(2,1)S(1)}, u32[]{:S(2)}, u32[]{:S(2)}) async-start(bf16[1,1,128,16]{3,1,0,2:T(2,128)(2,1)} %bitcast), calls=%async_computation | async-start | bytes 131072 | tf_op jit(solution)/shard_map/all_to_all | solution.py:84
  21.2 1.0 bitcast_convert_fusion.2
  22.9 0.6 subtract_exponential_fusion.1
  24.5 1.2 add_convert_fusion.14
  25.6 2.9 %collective-permute-start = (bf16[16,64,128]{2,1,0:T(8,128)(2,1)}, bf16[16,64,128]{2,1,0:T(8,128)(2,1)}, u32[]{:S(2)}, u32[]{:S(2)}) collective-permute-start(bf16[16,64,128]{2,1,0:T(8,128)(2,1)} %get-tuple-element.20), channel_id=1, source_target_pairs={{64,0},{128,64},{192,128},{256,192},{320,256},{384,320},{448,384},... | collective-permute-start | bytes 786440 | tf_op jit(solution)/shard_map/ppermute | solution.py:14
  29.2 6.0 %all-to-all-done = bf16[1,1,128,16]{3,1,0,2:T(2,128)(2,1)S(1)} async-done(((bf16[1,1,128,16]{3,1,0,2:T(2,128)(2,1)}), bf16[1,1,128,16]{3,1,0,2:T(2,128)(2,1)S(1)}, u32[]{:S(2)}, u32[]{:S(2)}) %all-to-all-start) | async-done | bytes 4128 | tf_op jit(solution)/shard_map/all_to_all | solution.py:84
  35.2 8.9 %all-to-all-start.1 = ((bf16[64,2,128]{2,1,0:T(2,128)(2,1)}), bf16[64,2,128]{2,1,0:T(2,128)(2,1)S(1)}, u32[]{:S(2)}, u32[]{:S(2)}) async-start(bf16[64,2,128]{2,1,0:T(2,128)(2,1)} %bitcast.172), calls=%async_computation.1 | async-start | bytes 65536 | tf_op jit(solution)/shard_map/all_to_all | solution.py:83
  45.3 2.1 reduce.4
  47.4 0.8 reshape.210
  49.2 8.4 %all-to-all-done.1 = bf16[64,2,128]{2,1,0:T(2,128)(2,1)S(1)} async-done(((bf16[64,2,128]{2,1,0:T(2,128)(2,1)}), bf16[64,2,128]{2,1,0:T(2,128)(2,1)S(1)}, u32[]{:S(2)}, u32[]{:S(2)}) %all-to-all-start.1) | async-done | bytes 32800 | tf_op jit(solution)/shard_map/all_to_all | solution.py:83
  57.6 6.1 %all-to-all-start.3 = ((bf16[64,2,1024]{2,1,0:T(2,128)(2,1)}), bf16[64,2,1024]{2,1,0:T(2,128)(2,1)S(1)}, u32[]{:S(2)}, u32[]{:S(2)}) async-start(bf16[64,2,1024]{2,1,0:T(2,128)(2,1)} %reshape.210), calls=%async_computation.3 | async-start | bytes 524288 | tf_op jit(solution)/shard_map/all_to_all | solution.py:81
  64.6 0.6 subtract_exponential_fusion
  66.0 18.8 %all-to-all-done.3 = bf16[64,2,1024]{2,1,0:T(2,128)(2,1)S(1)} async-done(((bf16[64,2,1024]{2,1,0:T(2,128)(2,1)}), bf16[64,2,1024]{2,1,0:T(2,128)(2,1)S(1)}, u32[]{:S(2)}, u32[]{:S(2)}) %all-to-all-start.3) | async-done | bytes 262176 | tf_op jit(solution)/shard_map/all_to_all | solution.py:81
  84.8 6.1 %all-to-all-start.2 = ((bf16[64,2,128]{2,1,0:T(2,128)(2,1)}), bf16[64,2,128]{2,1,0:T(2,128)(2,1)}, u32[]{:S(2)}, u32[]{:S(2)}) async-start(bf16[64,2,128]{2,1,0:T(2,128)(2,1)} %bitcast.173), calls=%async_computation.2 | async-start | bytes 65536 | tf_op jit(solution)/shard_map/all_to_all | solution.py:82
  91.1 1.5 bitcast_reduce_fusion.1
  93.9 3.6 %collective-permute-start.7 = (bf16[16,64,128]{2,1,0:T(8,128)(2,1)S(1)}, bf16[16,64,128]{2,1,0:T(8,128)(2,1)}, u32[]{:S(2)}, u32[]{:S(2)}) collective-permute-start(bf16[16,64,128]{2,1,0:T(8,128)(2,1)S(1)} %get-tuple-element.22), channel_id=1, source_target_pairs={{64,0},{128,64},{192,128},{256,192},{320,256},{384,320},{448,384},... | collective-permute-start | bytes 786440 | tf_op jit(solution)/shard_map/ppermute | solution.py:14
  97.6 1.2 fusion.9
  99.1 2.1 reduce.5
  101.2 0.8 reshape.216
  102.6 1.8 add_convert_fusion.13
  104.4 1.9 collective-permute-start.1
  106.4 0.6 copy-done.14
  107.0 1.8 add_convert_fusion.6
  108.8 2.0 collective-permute-start.8
  110.9 14.7 %all-to-all-start.5 = ((bf16[64,2,1024]{2,1,0:T(2,128)(2,1)}), bf16[64,2,1024]{2,1,0:T(2,128)(2,1)S(1)}, u32[]{:S(2)}, u32[]{:S(2)}) async-start(bf16[64,2,1024]{2,1,0:T(2,128)(2,1)} %reshape.216), calls=%async_computation.5 | async-start | bytes 524288 | tf_op jit(solution)/shard_map/all_to_all | solution.py:80
  126.6 0.7 copy-done.8
  127.5 0.8 reshape.215
  128.3 1.1 add_convert_fusion.12
  129.4 1.9 collective-permute-start.2
  131.4 1.1 add_convert_fusion.5
  132.5 1.9 collective-permute-start.9
  134.5 3.2 %collective-permute-done.2 = bf16[16,64,128]{2,1,0:T(8,128)(2,1)S(1)} collective-permute-done((bf16[16,64,128]{2,1,0:T(8,128)(2,1)S(1)}, bf16[16,64,128]{2,1,0:T(8,128)(2,1)S(1)}, u32[]{:S(2)}, u32[]{:S(2)}) %collective-permute-start.2) | collective-permute-done | bytes 262176 | tf_op jit(solution)/shard_map/ppermute | solution.py:14
  137.9 1.9 collective-permute-start.3
  139.8 7.4 %all-to-all-done.5 = bf16[64,2,1024]{2,1,0:T(2,128)(2,1)S(1)} async-done(((bf16[64,2,1024]{2,1,0:T(2,128)(2,1)}), bf16[64,2,1024]{2,1,0:T(2,128)(2,1)S(1)}, u32[]{:S(2)}, u32[]{:S(2)}) %all-to-all-start.5) | async-done | bytes 262176 | tf_op jit(solution)/shard_map/all_to_all | solution.py:80
  147.4 1.8 add_convert_fusion.4
  149.2 1.9 collective-permute-start.10
  151.2 1.5 bitcast_reduce_fusion
  154.5 4.5 %collective-permute-done.10 = bf16[16,64,128]{2,1,0:T(8,128)(2,1)} collective-permute-done((bf16[16,64,128]{2,1,0:T(8,128)(2,1)}, bf16[16,64,128]{2,1,0:T(8,128)(2,1)}, u32[]{:S(2)}, u32[]{:S(2)}) %collective-permute-start.10) | collective-permute-done | bytes 262176 | tf_op jit(solution)/shard_map/ppermute | solution.py:14
  159.0 1.8 add_convert_fusion.3
  160.8 1.9 collective-permute-start.11
  163.8 5.1 %collective-permute-done.11 = bf16[16,64,128]{2,1,0:T(8,128)(2,1)} collective-permute-done((bf16[16,64,128]{2,1,0:T(8,128)(2,1)}, bf16[16,64,128]{2,1,0:T(8,128)(2,1)}, u32[]{:S(2)}, u32[]{:S(2)}) %collective-permute-start.11) | collective-permute-done | bytes 262176 | tf_op jit(solution)/shard_map/ppermute | solution.py:14
  168.8 1.1 add_convert_fusion.2
  169.9 1.9 collective-permute-start.12
  172.0 1.1 add_convert_fusion.10
  173.1 1.9 collective-permute-start.4
  175.0 2.6 %collective-permute-done.12 = bf16[16,64,128]{2,1,0:T(8,128)(2,1)S(1)} collective-permute-done((bf16[16,64,128]{2,1,0:T(8,128)(2,1)S(1)}, bf16[16,64,128]{2,1,0:T(8,128)(2,1)S(1)}, u32[]{:S(2)}, u32[]{:S(2)}) %collective-permute-start.12) | collective-permute-done | bytes 262176 | tf_op jit(solution)/shard_map/ppermute | solution.py:14
  177.6 0.8 add_convert_fusion.1
  178.4 1.9 collective-permute-start.13
  180.5 0.7 copy.211
  181.2 6.1 %all-to-all-start.7 = ((bf16[1,64,2,128]{3,2,0,1:T(2,128)(2,1)}), bf16[1,64,2,128]{3,2,0,1:T(2,128)(2,1)S(1)}, u32[]{:S(2)}, u32[]{:S(2)}) async-start(bf16[1,64,2,128]{3,2,0,1:T(2,128)(2,1)} %bitcast.166), calls=%async_computation.7 | async-start | bytes 65536 | tf_op jit(solution)/shard_map/all_to_all | solution.py:133
  187.3 0.8 add_convert_fusion.9
  188.2 1.9 collective-permute-start.5
  190.6 0.6 copy.212
  191.2 9.5 %all-to-all-done.7 = bf16[1,64,2,128]{3,2,0,1:T(2,128)(2,1)S(1)} async-done(((bf16[1,64,2,128]{3,2,0,1:T(2,128)(2,1)}), bf16[1,64,2,128]{3,2,0,1:T(2,128)(2,1)S(1)}, u32[]{:S(2)}, u32[]{:S(2)}) %all-to-all-start.7) | async-done | bytes 32800 | tf_op jit(solution)/shard_map/all_to_all | solution.py:133
  200.7 5.1 %all-to-all-start.6 = ((bf16[1,64,2,128]{3,2,0,1:T(2,128)(2,1)}), bf16[1,64,2,128]{3,2,0,1:T(2,128)(2,1)S(1)}, u32[]{:S(2)}, u32[]{:S(2)}) async-start(bf16[1,64,2,128]{3,2,0,1:T(2,128)(2,1)} %bitcast.167), calls=%async_computation.6 | async-start | bytes 65536 | tf_op jit(solution)/shard_map/all_to_all | solution.py:132
  206.6 1.0 copy.174
  207.6 11.6 %all-to-all-done.6 = bf16[1,64,2,128]{3,2,0,1:T(2,128)(2,1)S(1)} async-done(((bf16[1,64,2,128]{3,2,0,1:T(2,128)(2,1)}), bf16[1,64,2,128]{3,2,0,1:T(2,128)(2,1)S(1)}, u32[]{:S(2)}, u32[]{:S(2)}) %all-to-all-start.6) | async-done | bytes 32800 | tf_op jit(solution)/shard_map/all_to_all | solution.py:132
  219.2 4.6 %all-to-all-start.4 = ((bf16[1,64,2,1024]{3,2,0,1:T(2,128)(2,1)}), bf16[1,64,2,1024]{3,2,0,1:T(2,128)(2,1)S(1)}, u32[]{:S(2)}, u32[]{:S(2)}) async-start(bf16[1,64,2,1024]{3,2,0,1:T(2,128)(2,1)} %copy.174), calls=%async_computation.4 | async-start | bytes 524288 | tf_op jit(solution)/shard_map/all_to_all | solution.py:131
  224.0 2.1 collective-permute-start.6
  226.3 0.8 fusion.22
  227.0 7.5 %collective-permute-done.6 = bf16[16,64,128]{2,1,0:T(8,128)(2,1)S(1)} collective-permute-done((bf16[16,64,128]{2,1,0:T(8,128)(2,1)S(1)}, bf16[16,64,128]{2,1,0:T(8,128)(2,1)S(1)}, u32[]{:S(2)}, u32[]{:S(2)}) %collective-permute-start.6) | collective-permute-done | bytes 262176 | tf_op jit(solution)/shard_map/ppermute | solution.py:14
  236.3 8.5 %all-to-all-done.4 = bf16[1,64,2,1024]{3,2,0,1:T(2,128)(2,1)S(1)} async-done(((bf16[1,64,2,1024]{3,2,0,1:T(2,128)(2,1)}), bf16[1,64,2,1024]{3,2,0,1:T(2,128)(2,1)S(1)}, u32[]{:S(2)}, u32[]{:S(2)}) %all-to-all-start.4) | async-done | bytes 262176 | tf_op jit(solution)/shard_map/all_to_all | solution.py:131
  245.8 0.8 copy.191
  (113 shorter events, 17.7 us)
Async XLA Ops:
  2.1 33.1 %all-to-all-start = ((bf16[1,1,128,16]{3,1,0,2:T(2,128)(2,1)}), bf16[1,1,128,16]{3,1,0,2:T(2,128)(2,1)S(1)}, u32[]{:S(2)}, u32[]{:S(2)}) async-start(bf16[1,1,128,16]{3,1,0,2:T(2,128)(2,1)} %bitcast), calls=%async_computation | async-start | bytes 131072 | tf_op jit(solution)/shard_map/all_to_all | solution.py:84
  21.2 2.4 copy-start
  23.6 0.8 copy-start.4
  25.6 76.4 %collective-permute-start = (bf16[16,64,128]{2,1,0:T(8,128)(2,1)}, bf16[16,64,128]{2,1,0:T(8,128)(2,1)}, u32[]{:S(2)}, u32[]{:S(2)}) collective-permute-start(bf16[16,64,128]{2,1,0:T(8,128)(2,1)} %get-tuple-element.20), channel_id=1, source_target_pairs={{64,0},{128,64},{192,128},{256,192},{320,256},{384,320},{448,384},... | collective-permute-start | bytes 786440 | tf_op jit(solution)/shard_map/ppermute | solution.py:14
  35.2 8.9 %copy-start.5 = (bf16[1,1,128,128]{3,2,1,0:T(8,128)(2,1)S(1)}, bf16[1,1,128,128]{3,2,1,0:T(8,128)(2,1)}, u32[]{:S(2)}) copy-start(bf16[1,1,128,128]{3,2,1,0:T(8,128)(2,1)} %param.9) | copy-start | bytes 98308
  35.2 22.4 %all-to-all-start.1 = ((bf16[64,2,128]{2,1,0:T(2,128)(2,1)}), bf16[64,2,128]{2,1,0:T(2,128)(2,1)S(1)}, u32[]{:S(2)}, u32[]{:S(2)}) async-start(bf16[64,2,128]{2,1,0:T(2,128)(2,1)} %bitcast.172), calls=%async_computation.1 | async-start | bytes 65536 | tf_op jit(solution)/shard_map/all_to_all | solution.py:83
  47.4 1.0 copy-start.1
  48.5 49.1 %copy-start.9 = (bf16[1,1,128,1024]{2,3,1,0:T(8,128)(2,1)}, bf16[1,1,128,1024]{2,3,1,0:T(8,128)(2,1)S(1)}, u32[]{:S(2)}) copy-start(bf16[1,1,128,1024]{2,3,1,0:T(8,128)(2,1)S(1)} %copy.176) | copy-start | bytes 786436
  49.2 48.4 %copy-start.16 = (pred[128,128]{1,0:T(8,128)(4,1)}, pred[128,128]{1,0:T(8,128)(4,1)S(1)}, u32[]{:S(2)}) copy-start(pred[128,128]{1,0:T(8,128)(4,1)S(1)} %iota_compare_fusion) | copy-start | bytes 49156
  57.6 27.1 %all-to-all-start.3 = ((bf16[64,2,1024]{2,1,0:T(2,128)(2,1)}), bf16[64,2,1024]{2,1,0:T(2,128)(2,1)S(1)}, u32[]{:S(2)}, u32[]{:S(2)}) async-start(bf16[64,2,1024]{2,1,0:T(2,128)(2,1)} %reshape.210), calls=%async_computation.3 | async-start | bytes 524288 | tf_op jit(solution)/shard_map/all_to_all | solution.py:81
  84.8 26.1 %all-to-all-start.2 = ((bf16[64,2,128]{2,1,0:T(2,128)(2,1)}), bf16[64,2,128]{2,1,0:T(2,128)(2,1)}, u32[]{:S(2)}, u32[]{:S(2)}) async-start(bf16[64,2,128]{2,1,0:T(2,128)(2,1)} %bitcast.173), calls=%async_computation.2 | async-start | bytes 65536 | tf_op jit(solution)/shard_map/all_to_all | solution.py:82
  93.9 12.4 %collective-permute-start.7 = (bf16[16,64,128]{2,1,0:T(8,128)(2,1)S(1)}, bf16[16,64,128]{2,1,0:T(8,128)(2,1)}, u32[]{:S(2)}, u32[]{:S(2)}) collective-permute-start(bf16[16,64,128]{2,1,0:T(8,128)(2,1)S(1)} %get-tuple-element.22), channel_id=1, source_target_pairs={{64,0},{128,64},{192,128},{256,192},{320,256},{384,320},{448,384},... | collective-permute-start | bytes 786440 | tf_op jit(solution)/shard_map/ppermute | solution.py:14
  102.0 0.6 copy-start.12
  104.4 23.9 %collective-permute-start.1 = (bf16[16,64,128]{2,1,0:T(8,128)(2,1)}, bf16[16,64,128]{2,1,0:T(8,128)(2,1)}, u32[]{:S(2)}, u32[]{:S(2)}) collective-permute-start(bf16[16,64,128]{2,1,0:T(8,128)(2,1)} %add_convert_fusion.13), channel_id=1, source_target_pairs={{64,0},{128,64},{192,128},{256,192},{320,256},{384,320},{448,384},... | collective-permute-start | bytes 786440 | tf_op jit(solution)/shard_map/ppermute | solution.py:14
  106.4 0.7 copy-start.14
  108.8 16.8 %copy-start.2 = (f32[1,1,16,64,128]{4,3,2,1,0:T(8,128)S(1)}, f32[1,1,16,64,128]{4,3,2,1,0:T(8,128)}, u32[]{:S(2)}) copy-start(f32[1,1,16,64,128]{4,3,2,1,0:T(8,128)} %param.12) | copy-start | bytes 1572868
  108.8 22.6 %collective-permute-start.8 = (bf16[16,64,128]{2,1,0:T(8,128)(2,1)}, bf16[16,64,128]{2,1,0:T(8,128)(2,1)}, u32[]{:S(2)}, u32[]{:S(2)}) collective-permute-start(bf16[16,64,128]{2,1,0:T(8,128)(2,1)} %add_convert_fusion.6), channel_id=1, source_target_pairs={{64,0},{128,64},{192,128},{256,192},{320,256},{384,320},{448,384},... | collective-permute-start | bytes 786440 | tf_op jit(solution)/shard_map/ppermute | solution.py:14
  110.9 36.3 %all-to-all-start.5 = ((bf16[64,2,1024]{2,1,0:T(2,128)(2,1)}), bf16[64,2,1024]{2,1,0:T(2,128)(2,1)S(1)}, u32[]{:S(2)}, u32[]{:S(2)}) async-start(bf16[64,2,1024]{2,1,0:T(2,128)(2,1)} %reshape.216), calls=%async_computation.5 | async-start | bytes 524288 | tf_op jit(solution)/shard_map/all_to_all | solution.py:80
  125.6 0.8 copy-start.7
  126.5 0.9 copy-start.8
  129.4 8.3 %collective-permute-start.2 = (bf16[16,64,128]{2,1,0:T(8,128)(2,1)S(1)}, bf16[16,64,128]{2,1,0:T(8,128)(2,1)S(1)}, u32[]{:S(2)}, u32[]{:S(2)}) collective-permute-start(bf16[16,64,128]{2,1,0:T(8,128)(2,1)S(1)} %add_convert_fusion.12), channel_id=1, source_target_pairs={{64,0},{128,64},{192,128},{256,192},{320,256},{384,320},{448,384},... | collective-permute-start | bytes 786440 | tf_op jit(solution)/shard_map/ppermute | solution.py:14
  132.5 15.0 %collective-permute-start.9 = (bf16[16,64,128]{2,1,0:T(8,128)(2,1)S(1)}, bf16[16,64,128]{2,1,0:T(8,128)(2,1)}, u32[]{:S(2)}, u32[]{:S(2)}) collective-permute-start(bf16[16,64,128]{2,1,0:T(8,128)(2,1)S(1)} %add_convert_fusion.5), channel_id=1, source_target_pairs={{64,0},{128,64},{192,128},{256,192},{320,256},{384,320},{448,384},... | collective-permute-start | bytes 786440 | tf_op jit(solution)/shard_map/ppermute | solution.py:14
  137.8 9.6 %copy-start.15 = (f32[16]{0:T(128)S(1)}, f32[16]{0:T(128)}, u32[]{:S(2)}) copy-start(f32[16]{0:T(128)} %get-tuple-element.14) | copy-start | bytes 196
  137.9 34.1 %collective-permute-start.3 = (bf16[16,64,128]{2,1,0:T(8,128)(2,1)S(1)}, bf16[16,64,128]{2,1,0:T(8,128)(2,1)}, u32[]{:S(2)}, u32[]{:S(2)}) collective-permute-start(bf16[16,64,128]{2,1,0:T(8,128)(2,1)S(1)} %add_convert_fusion.11), channel_id=1, source_target_pairs={{64,0},{128,64},{192,128},{256,192},{320,256},{384,320},{448,384},... | collective-permute-start | bytes 786440 | tf_op jit(solution)/shard_map/ppermute | solution.py:14
  149.2 9.8 %collective-permute-start.10 = (bf16[16,64,128]{2,1,0:T(8,128)(2,1)}, bf16[16,64,128]{2,1,0:T(8,128)(2,1)}, u32[]{:S(2)}, u32[]{:S(2)}) collective-permute-start(bf16[16,64,128]{2,1,0:T(8,128)(2,1)} %add_convert_fusion.4), channel_id=1, source_target_pairs={{64,0},{128,64},{192,128},{256,192},{320,256},{384,320},{448,384},... | collective-permute-start | bytes 786440 | tf_op jit(solution)/shard_map/ppermute | solution.py:14
  153.2 0.7 copy-start.17
  154.5 8.3 %copy-start.3 = (f32[1,1,16,64,128]{4,3,2,1,0:T(8,128)S(1)}, f32[1,1,16,64,128]{4,3,2,1,0:T(8,128)}, u32[]{:S(2)}) copy-start(f32[1,1,16,64,128]{4,3,2,1,0:T(8,128)} %param.13) | copy-start | bytes 1572868
  160.8 8.0 %collective-permute-start.11 = (bf16[16,64,128]{2,1,0:T(8,128)(2,1)}, bf16[16,64,128]{2,1,0:T(8,128)(2,1)}, u32[]{:S(2)}, u32[]{:S(2)}) collective-permute-start(bf16[16,64,128]{2,1,0:T(8,128)(2,1)} %add_convert_fusion.3), channel_id=1, source_target_pairs={{64,0},{128,64},{192,128},{256,192},{320,256},{384,320},{448,384},... | collective-permute-start | bytes 786440 | tf_op jit(solution)/shard_map/ppermute | solution.py:14
  169.9 2.1 copy-start.13
  169.9 7.7 %collective-permute-start.12 = (bf16[16,64,128]{2,1,0:T(8,128)(2,1)S(1)}, bf16[16,64,128]{2,1,0:T(8,128)(2,1)S(1)}, u32[]{:S(2)}, u32[]{:S(2)}) collective-permute-start(bf16[16,64,128]{2,1,0:T(8,128)(2,1)S(1)} %add_convert_fusion.2), channel_id=1, source_target_pairs={{64,0},{128,64},{192,128},{256,192},{320,256},{384,320},{448,384},... | collective-permute-start | bytes 786440 | tf_op jit(solution)/shard_map/ppermute | solution.py:14
  173.1 14.2 %collective-permute-start.4 = (bf16[16,64,128]{2,1,0:T(8,128)(2,1)S(1)}, bf16[16,64,128]{2,1,0:T(8,128)(2,1)S(1)}, u32[]{:S(2)}, u32[]{:S(2)}) collective-permute-start(bf16[16,64,128]{2,1,0:T(8,128)(2,1)S(1)} %add_convert_fusion.10), channel_id=1, source_target_pairs={{64,0},{128,64},{192,128},{256,192},{320,256},{384,320},{448,384},... | collective-permute-start | bytes 786440 | tf_op jit(solution)/shard_map/ppermute | solution.py:14
  178.4 11.6 %collective-permute-start.13 = (bf16[16,64,128]{2,1,0:T(8,128)(2,1)}, bf16[16,64,128]{2,1,0:T(8,128)(2,1)S(1)}, u32[]{:S(2)}, u32[]{:S(2)}) collective-permute-start(bf16[16,64,128]{2,1,0:T(8,128)(2,1)} %add_convert_fusion.1), channel_id=1, source_target_pairs={{64,0},{128,64},{192,128},{256,192},{320,256},{384,320},{448,384},... | collective-permute-start | bytes 786440 | tf_op jit(solution)/shard_map/ppermute | solution.py:14
  181.2 19.5 %all-to-all-start.7 = ((bf16[1,64,2,128]{3,2,0,1:T(2,128)(2,1)}), bf16[1,64,2,128]{3,2,0,1:T(2,128)(2,1)S(1)}, u32[]{:S(2)}, u32[]{:S(2)}) async-start(bf16[1,64,2,128]{3,2,0,1:T(2,128)(2,1)} %bitcast.166), calls=%async_computation.7 | async-start | bytes 65536 | tf_op jit(solution)/shard_map/all_to_all | solution.py:133
  188.2 35.6 %collective-permute-start.5 = (bf16[16,64,128]{2,1,0:T(8,128)(2,1)}, bf16[16,64,128]{2,1,0:T(8,128)(2,1)S(1)}, u32[]{:S(2)}, u32[]{:S(2)}) collective-permute-start(bf16[16,64,128]{2,1,0:T(8,128)(2,1)} %add_convert_fusion.9), channel_id=1, source_target_pairs={{64,0},{128,64},{192,128},{256,192},{320,256},{384,320},{448,384},... | collective-permute-start | bytes 786440 | tf_op jit(solution)/shard_map/ppermute | solution.py:14
  200.7 18.5 %all-to-all-start.6 = ((bf16[1,64,2,128]{3,2,0,1:T(2,128)(2,1)}), bf16[1,64,2,128]{3,2,0,1:T(2,128)(2,1)S(1)}, u32[]{:S(2)}, u32[]{:S(2)}) async-start(bf16[1,64,2,128]{3,2,0,1:T(2,128)(2,1)} %bitcast.167), calls=%async_computation.6 | async-start | bytes 65536 | tf_op jit(solution)/shard_map/all_to_all | solution.py:132
  219.2 25.6 %all-to-all-start.4 = ((bf16[1,64,2,1024]{3,2,0,1:T(2,128)(2,1)}), bf16[1,64,2,1024]{3,2,0,1:T(2,128)(2,1)S(1)}, u32[]{:S(2)}, u32[]{:S(2)}) async-start(bf16[1,64,2,1024]{3,2,0,1:T(2,128)(2,1)} %copy.174), calls=%async_computation.4 | async-start | bytes 524288 | tf_op jit(solution)/shard_map/all_to_all | solution.py:131
  223.8 2.2 copy-start.11
  224.0 2.3 copy-start.6
  224.0 10.5 %copy-start.10 = (bf16[1,1,128,1024]{2,3,1,0:T(8,128)(2,1)S(1)}, bf16[1,1,128,1024]{2,3,1,0:T(8,128)(2,1)}, u32[]{:S(2)}) copy-start(bf16[1,1,128,1024]{2,3,1,0:T(8,128)(2,1)} %copy-done.9) | copy-start | bytes 786436
  224.0 10.5 %collective-permute-start.6 = (bf16[16,64,128]{2,1,0:T(8,128)(2,1)S(1)}, bf16[16,64,128]{2,1,0:T(8,128)(2,1)S(1)}, u32[]{:S(2)}, u32[]{:S(2)}) collective-permute-start(bf16[16,64,128]{2,1,0:T(8,128)(2,1)S(1)} %add_convert_fusion.8), channel_id=1, source_target_pairs={{64,0},{128,64},{192,128},{256,192},{320,256},{384,320},{448,384},... | collective-permute-start | bytes 786440 | tf_op jit(solution)/shard_map/ppermute | solution.py:14
where the time goes:
time: 252 us; the launch traced here: 247 us
  starting transfers between devices  101 us (40%)
  waiting for transfers between devices  93.1 us (37%)
  other arithmetic  22.6 us (9%)
  local copies, waits for them, and re-layouts  21.2 us (8%)
  matrix products  7.8 us (3%)
    ppermute x14, starting transfers between devices, shifted(): return lax.ppermute(x, axis, pairs)  29.7 us
    ppermute x14, waiting for transfers between devices, shifted(): return lax.ppermute(x, axis, pairs)  22.9 us
    all_to_all x1, starting transfers between devices, shards(): lax.all_to_all(decay_last, 'tiles', split_axis=2, concat_axis=1, tiled=True)  19.1 us
    all_to_all x1, waiting for transfers between devices, shards(): lax.all_to_all(grad_out, 'tiles', split_axis=2, concat_axis=1, tiled=True)  18.8 us
    all_to_all x1, starting transfers between devices, shards(): lax.all_to_all(inputs, 'tiles', split_axis=2, concat_axis=1, tiled=True)  14.7 us
    unnamed x55, local copies, waits for them, and re-layouts  11.9 us
    all_to_all x1, waiting for transfers between devices, shards(): lax.all_to_all(to_columns(col_grad_b), 'tiles', split_axis=1, concat_axis...  11.6 us
    all_to_all x1, waiting for transfers between devices, shards(): lax.all_to_all(to_columns(col_grad_c), 'tiles', split_axis=1, concat_axis...  9.48 us
  transfers between devices with their start and end apart: 22, of which 12 were waited for; matrix products, arithmetic and copies ran while one was open for 18% of the time, Pallas kernels for 0%

commit v1 on v0

v1 whole, which is shorter than its diff:
```python
import jax
import jax.numpy as jnp
from jax import lax
from jax.experimental import pallas as pl
from jax.experimental.pallas import tpu as pltpu
from jax.sharding import PartitionSpec as P

HEADS = 16
HEAD_DIM = 64
STATE = 128
TOKENS = 128
CHANNELS = 1024
LANES = 128
PAIRS = CHANNELS // LANES
TILES = 64
DEPTH_Z = 16
DEPTH_X = 4
FRAMES = 8
HALF = PAIRS // 2
EARLY = 12
PER_HOP = 9
BF = jnp.bfloat16
F32 = jnp.float32
MESH = pl.DeviceIdType.MESH


def nn(a, b):
    return lax.dot_general(a, b, (((1,), (0,)), ((), ())), preferred_element_type=F32)


def nt(a, b):
    return lax.dot_general(a, b, (((1,), (1,)), ((), ())), preferred_element_type=F32)


def iota(shape, dim):
    return lax.broadcasted_iota(jnp.int32, shape, dim)


def ones_where(cond):
    return jnp.where(cond, 1.0, 0.0).astype(BF)


def square(shape=(TOKENS, TOKENS)):
    return iota(shape, 0), iota(shape, 1)


def place(index, column_order):
    if not column_order:
        return index
    return lax.shift_left(index & 1, 6) + lax.shift_right_logical(index, 1)


def causal(column_order):
    t, s = square()
    return place(s, column_order) <= place(t, column_order)


def causal_transposed(column_order):
    s, t = square()
    return place(s, column_order) <= place(t, column_order)


def high(index, bits):
    return lax.shift_right_logical(index, bits)


def interleave(back=False):
    r, c = square()
    if back:
        r, c = c, r
    return ones_where((high(r, 3) == (c & 15)) & ((r & 7) == high(c, 4)))


def identity():
    r, c = square()
    return ones_where(r == c)


def maps_matrix(bits, parts, back=False):
    shape = (16 << bits, 32 * parts)
    if back:
        c, r = square(shape[::-1])
    else:
        r, c = square(shape)
    part, token = high(c, 5), c & 31
    return ones_where(r == lax.shift_left(high(token, 1), bits) + part * 2 + (token & 1))


def pair(k):
    return slice(LANES * k, LANES * k + LANES)


def pack_channels(read, write):
    mix = interleave()
    for q in range(8):
        stack = jnp.concatenate([read(q, k) for k in range(PAIRS)], axis=0)
        write(q, nn(mix, stack).reshape(8, 2, 8, LANES).astype(BF))


def unpack_channels(read, write):
    mix = interleave(True)
    for q in range(8):
        tiles = read(q).astype(F32).reshape(TOKENS, LANES).astype(BF)
        out = nn(mix, tiles)
        for k in range(PAIRS):
            write(q, k, out[16 * k : 16 * k + 16, :])


def block_states(grad, c_rows, decays, column_order, refs, term, low):
    grow, ends, centred, headed = refs
    run = ones_where(causal(column_order))
    c_turned = nt(identity(), c_rows).astype(BF)
    head, channel = square((TOKENS, LANES))
    for k in range(PAIRS):
        spread = ones_where(high(channel, 6) + 2 * k == head)
        cum = nn(run, nn(decays, spread).astype(BF))
        total = cum[TOKENS - 1 : TOKENS, :]
        middle = total * 0.5
        to_middle = jnp.exp(middle)
        shrunk = grad[:, pair(k)].astype(F32) * jnp.exp(cum - middle)
        grow[:, pair(k)] = jnp.exp(middle - cum)
        ends[k, 0:1, :] = to_middle
        ends[k, 1:2, :] = jnp.exp(total)
        centred[:, pair(k)] = shrunk.astype(BF)
        by_head = (shrunk * to_middle).astype(BF)
        headed[:, pair(k)] = by_head
        state = nn(c_turned, by_head)
        term[k] = state
        low[k] = state.astype(BF)


def grad_of_x(b_rows, c_rows, carry, column_order, refs, tails, write):
    grow, ends, centred, headed = refs
    pairing = jnp.where(causal_transposed(column_order), nt(b_rows, c_rows), 0.0).astype(BF)
    both = jnp.concatenate([pairing, b_rows], axis=1)
    for k in range(PAIRS):
        tail = (carry[k].astype(F32) * ends[k, 0:1, :]).astype(BF)
        tails[:, pair(k)] = tail
        stack = jnp.concatenate([centred[:, pair(k)], tail], axis=0)
        write(k, nn(both, stack) * grow[:, pair(k)])


def grads_of_maps(x, b_rows, c_rows, saved, column_order, refs, tails, scaled):
    grow, ends, centred, headed = refs
    for k in range(PAIRS):
        scaled[:, pair(k)] = (x[:, pair(k)].astype(F32) * grow[:, pair(k)]).astype(BF)
    mixed = jnp.where(causal(column_order), nt(centred[...], scaled[...]), 0.0)
    part_b = nn(mixed.T.astype(BF), c_rows) + nt(scaled[...], tails[...])
    part_c = nn(mixed.astype(BF), b_rows) + nn(headed[...], saved[...].astype(BF))
    return part_b, part_c


def kernel(
    x_hbm, g_hbm, b_hbm, c_hbm, d_hbm, saved_row_hbm, saved_col_hbm,
    out_x, out_b, out_c,
    x_ref, g_ref, b_ref, c_ref, d_ref, saved_row, saved_col,
    send_g, send_x, got_g, got_x, back_x, back_m, home_x, home_m,
    row_grow, row_centred, row_headed, col_grow, col_centred, col_headed,
    term, low, ends, peer_low, peer_ends, incoming, outgoing, give, carry,
    tails, scaled, wide, col_maps, part_x,
    load_sem, send_sem, recv_sem, swap_send, swap_recv, hop_send, hop_recv, give_send, give_recv,
):
    f = lax.axis_index("frames")
    me = lax.axis_index("tiles")
    z, x = lax.div(me, DEPTH_X), lax.rem(me, DEPTH_X)

    loads = [
        pltpu.make_async_copy(source, target, load_sem.at[i])
        for i, (source, target) in enumerate([
            (g_hbm, g_ref), (b_hbm, b_ref), (c_hbm, c_ref), (d_hbm, d_ref), (x_hbm, x_ref),
            (saved_row_hbm, saved_row), (saved_col_hbm, saved_col),
        ])
    ]
    for load in loads:
        load.start()

    def partner(k):
        step = TILES - 1 - k
        u, dx = lax.div(step, DEPTH_X), lax.rem(step, DEPTH_X)
        dz = lax.div(u + 1, 2) * (2 * lax.rem(u, 2) - 1)
        return lax.rem(z + dz + DEPTH_Z, DEPTH_Z) * DEPTH_X + lax.rem(x + dx, DEPTH_X)

    barrier = pltpu.get_barrier_semaphore()

    @pl.loop(0, TILES - 1)
    def _(k):
        pl.semaphore_signal(barrier, inc=1, device_id=(f, partner(k)), device_id_type=MESH)

    core, chip_y = lax.rem(f, 2), lax.div(f, 2)
    other = f + 1 - 2 * core
    above, below = lax.rem(f + 2, FRAMES), lax.rem(f + FRAMES - 2, FRAMES)
    mine, theirs = core * HALF, HALF - core * HALF
    for neighbour in (other, above, below):
        pl.semaphore_signal(barrier, inc=1, device_id=(neighbour, me), device_id_type=MESH)

    def keep_own(source, target):
        target[pl.ds(me, 1)] = source[pl.ds(me, 1)]

    def exchange(source, target, which, first=0, last=TILES - 1):
        @pl.loop(first, last)
        def _(k):
            peer = partner(k)
            pltpu.make_async_remote_copy(
                src_ref=source.at[peer],
                dst_ref=target.at[me],
                send_sem=send_sem.at[which],
                recv_sem=recv_sem.at[which],
                device_id=(f, peer),
                device_id_type=MESH,
            ).start()

    def wait_all(ref, sem):
        some = ref.at[pl.ds(0, TILES - 1)]
        pltpu.make_async_copy(some, some, sem).wait()

    def put_g(q, value):
        send_g[8 * q : 8 * q + 8, 0:2] = value

    def put_x(q, value):
        send_x[8 * q : 8 * q + 8] = value

    def reader(ref):
        return lambda q, k: ref[16 * q : 16 * q + 16, pair(k)]

    loads[0].wait()
    pack_channels(reader(g_ref), put_g)
    for i in (1, 2, 3):
        loads[i].wait()
    decays = nt(identity(), jnp.concatenate(
        [d_ref[...], jnp.zeros((TOKENS - HEADS, TOKENS), BF)], axis=0)).astype(BF)
    b_rows, c_rows = b_ref[...], c_ref[...]
    spread_maps = maps_matrix(3, 3)
    for q in range(4):
        rows = slice(32 * q, 32 * q + 32)
        stack = jnp.concatenate([b_rows[rows], c_rows[rows], decays[rows]], axis=0)
        packed = nn(spread_maps, stack).reshape(16, 8, LANES).astype(BF)
        send_g[16 * q : 16 * q + 16, 2] = packed

    pl.semaphore_wait(barrier, TILES + 2)
    exchange(send_g, got_g, 0)
    keep_own(send_g, got_g)
    loads[4].wait()
    pack_channels(reader(x_ref), put_x)
    keep_own(send_x, got_x)

    @pl.when(chip_y == FRAMES // 2 - 1)
    def _():
        incoming[...] = jnp.zeros_like(incoming)

    def swap_copies(order):
        return [
            pltpu.make_async_remote_copy(
                src_ref=source,
                dst_ref=target,
                send_sem=swap_send.at[order, i],
                recv_sem=swap_recv.at[order, i],
                device_id=(other, me),
                device_id_type=MESH,
            )
            for i, (source, target) in enumerate([
                (ends.at[order], peer_ends.at[order]),
                (low.at[order, pl.ds(theirs, HALF)], peer_low.at[order]),
            ])
        ]

    def hop_copy(order, i):
        return pltpu.make_async_remote_copy(
            src_ref=outgoing.at[order, i],
            dst_ref=incoming.at[order, i],
            send_sem=hop_send.at[order, i],
            recv_sem=hop_recv.at[order, i],
            device_id=(below, me),
            device_id_type=MESH,
        )

    def give_copy(order, i):
        return pltpu.make_async_remote_copy(
            src_ref=give.at[order, i],
            dst_ref=carry.at[order, mine + i],
            send_sem=give_send.at[order, i],
            recv_sem=give_recv.at[order, i],
            device_id=(other, me),
            device_id_type=MESH,
        )

    def swapped(order):
        for copy in swap_copies(order):
            copy.wait_recv()

    def chain(order):
        for i in range(HALF):
            k = mine + i
            own_state, peer_state = term[order, k], peer_low[order, i].astype(F32)
            own_decay, peer_decay = ends[order, k, 1:2, :], peer_ends[order, k, 1:2, :]
            lower = core == 0
            lower_state = jnp.where(lower, own_state, peer_state)
            upper_state = jnp.where(lower, peer_state, own_state)
            lower_decay = jnp.where(lower, own_decay, peer_decay)
            upper_decay = jnp.where(lower, peer_decay, own_decay)

            @pl.when(chip_y < FRAMES // 2 - 1)
            def _():
                hop_copy(order, i).wait_recv()

            entering = incoming[order, i].astype(F32)
            between = upper_decay * entering + upper_state

            @pl.when(chip_y > 0)
            def _():
                outgoing[order, i] = (lower_decay * between + lower_state).astype(BF)
                hop_copy(order, i).start()

            carry[order, k] = jnp.where(lower, between, entering).astype(BF)
            give[order, i] = jnp.where(lower, entering, between).astype(BF)
            give_copy(order, i).start()

    def chain_end(order):
        for i in range(HALF):
            pltpu.make_async_copy(
                carry.at[order, theirs + i], carry.at[order, theirs + i], give_recv.at[order, i]
            ).wait()

    def chain_sent(order):
        for copy in swap_copies(order):
            copy.wait_send()
        for i in range(HALF):
            give_copy(order, i).wait_send()

            @pl.when(chip_y > 0)
            def _():
                hop_copy(order, i).wait_send()

    row_refs = (row_grow, ends.at[0], row_centred, row_headed)
    block_states(g_ref, c_rows, decays, False, row_refs, term.at[0], low.at[0])
    for copy in swap_copies(0):
        copy.start()

    wait_all(got_g, recv_sem.at[0])
    exchange(send_x, got_x, 1, 0, EARLY)

    def put_wide(q, k, value):
        wide[16 * q : 16 * q + 16, pair(k)] = value.astype(BF)

    unpack_channels(lambda q: got_g[8 * q : 8 * q + 8, 0:2], put_wide)
    gather_maps = maps_matrix(3, 3, True)
    for q in range(4):
        tiles = got_g[16 * q : 16 * q + 16, 2].astype(F32).reshape(TOKENS, LANES).astype(BF)
        piece = nn(gather_maps, tiles).astype(BF)
        for p in range(3):
            col_maps[p, 32 * q : 32 * q + 32] = piece[32 * p : 32 * p + 32]
    col_refs = (col_grow, ends.at[1], col_centred, col_headed)
    block_states(wide, col_maps[1], col_maps[2], True, col_refs, term.at[1], low.at[1])
    for copy in swap_copies(1):
        copy.start()
    filled = EARLY + PER_HOP * (FRAMES // 2 - 1 - chip_y)
    swapped(1)
    exchange(send_x, got_x, 1, EARLY, filled)
    chain(1)
    exchange(send_x, got_x, 1, filled)
    chain_end(1)

    def put_col(k, value):
        wide[:, pair(k)] = value.astype(BF)

    grad_of_x(col_maps[0], col_maps[1], carry.at[1], True, col_refs, tails, put_col)

    def put_back(q, value):
        back_x[8 * q : 8 * q + 8] = value

    pack_channels(reader(wide), put_back)
    swapped(0)
    chain(0)
    exchange(back_x, home_x, 2)
    keep_own(back_x, home_x)

    wait_all(got_x, recv_sem.at[1])
    loads[6].wait()
    unpack_channels(lambda q: got_x[8 * q : 8 * q + 8], put_wide)
    col_b, col_c = grads_of_maps(
        wide, col_maps[0], col_maps[1], saved_col, True, col_refs, tails, scaled)
    col_b, col_c = col_b.astype(BF), col_c.astype(BF)
    spread_back = maps_matrix(2, 2)
    for q in range(4):
        rows = slice(32 * q, 32 * q + 32)
        stack = jnp.concatenate([col_b[rows], col_c[rows]], axis=0)
        packed = nn(spread_back, stack).reshape(16, 4, LANES).astype(BF)
        back_m[16 * q : 16 * q + 16] = packed
    exchange(back_m, home_m, 3)
    keep_own(back_m, home_m)

    def put_row(k, value):
        part_x[:, pair(k)] = value

    chain_end(0)
    grad_of_x(b_rows, c_rows, carry.at[0], False, row_refs, tails, put_row)
    loads[5].wait()
    row_b, row_c = grads_of_maps(
        x_ref, b_rows, c_rows, saved_row, False, row_refs, tails, scaled)

    wait_all(home_x, recv_sem.at[2])

    def put_sum(q, k, value):
        rows = slice(16 * q, 16 * q + 16)
        out_x[rows, pair(k)] = (part_x[rows, pair(k)] + value).astype(BF)

    unpack_channels(lambda q: home_x[8 * q : 8 * q + 8], put_sum)

    wait_all(home_m, recv_sem.at[3])
    gather_back = maps_matrix(2, 2, True)
    for q in range(4):
        rows = slice(32 * q, 32 * q + 32)
        tiles = home_m[16 * q : 16 * q + 16].astype(F32).reshape(64, LANES).astype(BF)
        both = nn(gather_back, tiles)
        out_b[rows, :] = (row_b[rows] + both[0:32]).astype(BF)
        out_c[rows, :] = (row_c[rows] + both[32:64]).astype(BF)

    chain_sent(0)
    chain_sent(1)
    wait_all(send_g, send_sem.at[0])
    wait_all(send_x, send_sem.at[1])
    wait_all(back_x, send_sem.at[2])
    wait_all(back_m, send_sem.at[3])


def shards(inputs, grad_out, b_proj, c_proj, log_decay, saved_raster, saved_column):
    vmem = pl.BlockSpec(memory_space=pltpu.VMEM)
    out_x, out_b, out_c = pl.pallas_call(
        kernel,
        out_shape=(
            jax.ShapeDtypeStruct((TOKENS, CHANNELS), BF),
            jax.ShapeDtypeStruct((TOKENS, STATE), BF),
            jax.ShapeDtypeStruct((TOKENS, STATE), BF),
        ),
        in_specs=[pl.BlockSpec(memory_space=pltpu.HBM)] * 7,
        out_specs=(vmem, vmem, vmem),
        scratch_shapes=[
            pltpu.VMEM((TOKENS, CHANNELS), BF),
            pltpu.VMEM((TOKENS, CHANNELS), BF),
            pltpu.VMEM((TOKENS, STATE), BF),
            pltpu.VMEM((TOKENS, STATE), BF),
            pltpu.VMEM((HEADS, TOKENS), BF),
            pltpu.VMEM((CHANNELS, STATE), F32),
            pltpu.VMEM((CHANNELS, STATE), F32),
            pltpu.VMEM((TILES, 3, 8, LANES), BF),
            pltpu.VMEM((TILES, 2, 8, LANES), BF),
            pltpu.VMEM((TILES, 3, 8, LANES), BF),
            pltpu.VMEM((TILES, 2, 8, LANES), BF),
            pltpu.VMEM((TILES, 2, 8, LANES), BF),
            pltpu.VMEM((TILES, 4, LANES), BF),
            pltpu.VMEM((TILES, 2, 8, LANES), BF),
            pltpu.VMEM((TILES, 4, LANES), BF),
            pltpu.VMEM((TOKENS, CHANNELS), F32),
            pltpu.VMEM((TOKENS, CHANNELS), BF),
            pltpu.VMEM((TOKENS, CHANNELS), BF),
            pltpu.VMEM((TOKENS, CHANNELS), F32),
            pltpu.VMEM((TOKENS, CHANNELS), BF),
            pltpu.VMEM((TOKENS, CHANNELS), BF),
            pltpu.VMEM((2, PAIRS, STATE, LANES), F32),
            pltpu.VMEM((2, PAIRS, STATE, LANES), BF),
            pltpu.VMEM((2, PAIRS, 2, LANES), F32),
            pltpu.VMEM((2, HALF, STATE, LANES), BF),
            pltpu.VMEM((2, PAIRS, 2, LANES), F32),
            pltpu.VMEM((2, HALF, STATE, LANES), BF),
            pltpu.VMEM((2, HALF, STATE, LANES), BF),
            pltpu.VMEM((2, HALF, STATE, LANES), BF),
            pltpu.VMEM((2, PAIRS, STATE, LANES), BF),
            pltpu.VMEM((STATE, CHANNELS), BF),
            pltpu.VMEM((TOKENS, CHANNELS), BF),
            pltpu.VMEM((TOKENS, CHANNELS), BF),
            pltpu.VMEM((3, TOKENS, LANES), BF),
            pltpu.VMEM((TOKENS, CHANNELS), F32),
            pltpu.SemaphoreType.DMA((7,)),
            pltpu.SemaphoreType.DMA((4,)),
            pltpu.SemaphoreType.DMA((4,)),
            pltpu.SemaphoreType.DMA((2, 2)),
            pltpu.SemaphoreType.DMA((2, 2)),
            pltpu.SemaphoreType.DMA((2, HALF)),
            pltpu.SemaphoreType.DMA((2, HALF)),
            pltpu.SemaphoreType.DMA((2, HALF)),
            pltpu.SemaphoreType.DMA((2, HALF)),
        ],
        compiler_params=pltpu.CompilerParams(
            collective_id=0, has_side_effects=True, vmem_limit_bytes=63 * 1024 * 1024
        ),
        cost_estimate=pl.CostEstimate(
            flops=800_000_000, bytes_accessed=2_600_000, transcendentals=1_000_000
        ),
        name="scan_backward",
    )(
        inputs.reshape(TOKENS, CHANNELS),
        grad_out.reshape(TOKENS, CHANNELS),
        b_proj.reshape(TOKENS, STATE),
        c_proj.reshape(TOKENS, STATE),
        log_decay.reshape(HEADS, TOKENS),
        saved_raster.reshape(CHANNELS, STATE),
        saved_column.reshape(CHANNELS, STATE),
    )
    return (
        out_x.reshape(1, 1, TOKENS, CHANNELS),
        out_b.reshape(1, 1, TOKENS, STATE),
        out_c.reshape(1, 1, TOKENS, STATE),
    )


def solution(mesh):
    in_specs = (
        P("frames", "tiles", None, None),
        P("frames", "tiles", None, None),
        P("frames", "tiles", None, None),
        P("frames", "tiles", None, None),
        P(None, "frames", "tiles", None),
        P("frames", "tiles", None, None, None),
        P("frames", "tiles", None, None, None),
    )
    out_specs = (
        P("frames", "tiles", None, None),
        P("frames", "tiles", None, None),
        P("frames", "tiles", None, None),
    )
    return jax.shard_map(shards, mesh=mesh, in_specs=in_specs, out_specs=out_specs, check_vma=False)
```

time: 252 us -> 78.6 us (0.31); the launches traced: 247 us -> 78.4 us
  starting transfers between devices: 101 us -> 0 us
  waiting for transfers between devices: 93.1 us -> 0 us
  Pallas kernels: 0 us -> 74.7 us
  other arithmetic: 22.6 us -> 0 us
  local copies, waits for them, and re-layouts: 21.2 us -> 3.06 us
  matrix products: 7.8 us -> 0 us
    pallas_call x0 -> x1, Pallas kernels: none -> 74.7 us  [shards(): pl.pallas_call(kernel, out_shape=(jax.ShapeDtypeStruct((TOKENS, CHANNELS)...]
    all_to_all x8 -> x0, starting transfers between devices: 70.8 us -> none  [the longest x1 19.1 us: shards(): lax.all_to_all(decay_last, 'tiles', split_axis=2, concat_axis=1, tiled=True)]
    all_to_all x8 -> x0, waiting for transfers between devices: 70.2 us -> none  [the longest x1 18.8 us: shards(): lax.all_to_all(grad_out, 'tiles', split_axis=2, concat_axis=1, tiled=True)]
    ppermute x14 -> x0, starting transfers between devices: 29.7 us -> none  [shifted(): return lax.ppermute(x, axis, pairs)]
    ppermute x14 -> x0, waiting for transfers between devices: 22.9 us -> none  [shifted(): return lax.ppermute(x, axis, pairs)]
    convert_element_type x19 -> x0, other arithmetic: 15.7 us -> none  [the longest x6 8.38 us: shards(): leaving_state[1].astype(jnp.bfloat16)]
    unnamed x55 -> x7, local copies, waits for them, and re-layouts: 11.9 us -> 3.06 us
    dot_general x18 -> x0, matrix products: 7.8 us -> none  [the longest x2 1.69 us: block_grads(): jnp.einsum('tho,sho->hts', grad_heads, input_heads, preferred_element_typ...]
  transfers between devices with their start and end apart: 22 -> 0, of which waited for: 12 -> 0; matrix products, arithmetic and copies ran while one was open for 18% -> 0% of each run, Pallas kernels for 0% -> 0%
where the time goes in v1:
time: 78.6 us; the launch traced here: 78.4 us
  Pallas kernels  74.7 us (95%)
  local copies, waits for them, and re-layouts  3.06 us (4%)
    pallas_call x1, Pallas kernels, shards(): pl.pallas_call(kernel, out_shape=(jax.ShapeDtypeStruct((TOKENS, CHANNELS)...  74.7 us
    unnamed x7, local copies, waits for them, and re-layouts  3.06 us

profile of v1, /device:TPU:1, one launch (start us, length us, event | category | flops | bytes accessed | tf_op | source)
XLA Modules:
  0.0 78.4 jit_solution(17394766785284025128)
XLA Ops:
  0.6 74.7 %scan_backward.1 = (bf16[128,1024]{1,0:T(8,128)(2,1)}, bf16[128,128]{1,0:T(8,128)(2,1)}, bf16[128,128]{1,0:T(8,128)(2,1)}) custom-call(bf16[128,1024]{1,0:T(8,128)(2,1)} %bitcast.15, bf16[128,1024]{1,0:T(8,128)(2,1)} %bitcast.16, bf16[128,128]{1,0:T(8,128)(2,1)} %bitcast.17, bf16[128,128]{1,0:T(8,128)(2,1)} %bitcast.18, bf16[16,128]{1,0:T(8,128)(2,1)} %bitcast.19, ...), custom_call_target="tpu_custom_call" | custom-call | flops 800000000 | bytes 2600000 | tf_op jit(solution)/shard_map/scan_backward/pallas_call | solution.py:427
  75.3 0.0 copy-start.1
  75.3 1.7 %copy.13 = bf16[1,1,128,1024]{3,2,1,0:T(8,128)(2,1)} copy(bf16[1,1,128,1024]{3,2,1,0:T(8,128)(2,1)} %bitcast.10) | data formatting | bytes 524288
  77.0 0.0 copy-done.1
  77.0 0.0 copy-start
  77.0 0.6 copy.14
  77.6 0.2 copy-done
  77.8 0.6 copy.15
Async XLA Ops:
  75.3 1.7 %copy-start.1 = (bf16[128,128]{1,0:T(8,128)(2,1)S(1)}, bf16[128,128]{1,0:T(8,128)(2,1)}, u32[]{:S(2)}) copy-start(bf16[128,128]{1,0:T(8,128)(2,1)} %get-tuple-element.7) | copy-start | bytes 98308
  77.0 0.8 copy-start

commit v2 on v1

--- a/solution.py
+++ b/solution.py
@@ -17,8 +17,9 @@
 DEPTH_X = 4
 FRAMES = 8
 HALF = PAIRS // 2
-EARLY = 12
-PER_HOP = 9
+BEHIND = 8
+EARLY = 20
+PER_HOP = 7
 BF = jnp.bfloat16
 F32 = jnp.float32
 MESH = pl.DeviceIdType.MESH
@@ -106,23 +107,27 @@
             write(q, k, out[16 * k : 16 * k + 16, :])
 
 
-def block_states(grad, c_rows, decays, column_order, refs, term, low):
-    grow, ends, centred, headed = refs
+def block_scales(decays, column_order, shrink, grow, ends):
     run = ones_where(causal(column_order))
-    c_turned = nt(identity(), c_rows).astype(BF)
     head, channel = square((TOKENS, LANES))
     for k in range(PAIRS):
         spread = ones_where(high(channel, 6) + 2 * k == head)
         cum = nn(run, nn(decays, spread).astype(BF))
         total = cum[TOKENS - 1 : TOKENS, :]
         middle = total * 0.5
-        to_middle = jnp.exp(middle)
-        shrunk = grad[:, pair(k)].astype(F32) * jnp.exp(cum - middle)
+        shrink[:, pair(k)] = jnp.exp(cum - middle)
         grow[:, pair(k)] = jnp.exp(middle - cum)
-        ends[k, 0:1, :] = to_middle
+        ends[k, 0:1, :] = jnp.exp(middle)
         ends[k, 1:2, :] = jnp.exp(total)
+
+
+def block_states(grad, c_rows, shrink, refs, term, low):
+    grow, ends, centred, headed = refs
+    c_turned = nt(identity(), c_rows).astype(BF)
+    for k in range(PAIRS):
+        shrunk = grad[:, pair(k)].astype(F32) * shrink[:, pair(k)]
         centred[:, pair(k)] = shrunk.astype(BF)
-        by_head = (shrunk * to_middle).astype(BF)
+        by_head = (shrunk * ends[k, 0:1, :]).astype(BF)
         headed[:, pair(k)] = by_head
         state = nn(c_turned, by_head)
         term[k] = state
@@ -134,7 +139,7 @@
     pairing = jnp.where(causal_transposed(column_order), nt(b_rows, c_rows), 0.0).astype(BF)
     both = jnp.concatenate([pairing, b_rows], axis=1)
     for k in range(PAIRS):
-        tail = (carry[k].astype(F32) * ends[k, 0:1, :]).astype(BF)
+        tail = (carry(k).astype(F32) * ends[k, 0:1, :]).astype(BF)
         tails[:, pair(k)] = tail
         stack = jnp.concatenate([centred[:, pair(k)], tail], axis=0)
         write(k, nn(both, stack) * grow[:, pair(k)])
@@ -154,8 +159,8 @@
     x_hbm, g_hbm, b_hbm, c_hbm, d_hbm, saved_row_hbm, saved_col_hbm,
     out_x, out_b, out_c,
     x_ref, g_ref, b_ref, c_ref, d_ref, saved_row, saved_col,
-    send_g, send_x, got_g, got_x, back_x, back_m, home_x, home_m,
-    row_grow, row_centred, row_headed, col_grow, col_centred, col_headed,
+    send_m, send_g, send_x, got_m, got_g, got_x, back_x, back_m, home_x, home_m,
+    shrink, row_grow, row_centred, row_headed, col_grow, col_centred, col_headed,
     term, low, ends, peer_low, peer_ends, incoming, outgoing, give, carry,
     tails, scaled, wide, col_maps, part_x,
     load_sem, send_sem, recv_sem, swap_send, swap_recv, hop_send, hop_recv, give_send, give_recv,
@@ -214,7 +219,7 @@
         pltpu.make_async_copy(some, some, sem).wait()
 
     def put_g(q, value):
-        send_g[8 * q : 8 * q + 8, 0:2] = value
+        send_g[8 * q : 8 * q + 8] = value
 
     def put_x(q, value):
         send_x[8 * q : 8 * q + 8] = value
@@ -222,8 +227,6 @@
     def reader(ref):
         return lambda q, k: ref[16 * q : 16 * q + 16, pair(k)]
 
-    loads[0].wait()
-    pack_channels(reader(g_ref), put_g)
     for i in (1, 2, 3):
         loads[i].wait()
     decays = nt(identity(), jnp.concatenate(
@@ -234,14 +237,15 @@
         rows = slice(32 * q, 32 * q + 32)
         stack = jnp.concatenate([b_rows[rows], c_rows[rows], decays[rows]], axis=0)
         packed = nn(spread_maps, stack).reshape(16, 8, LANES).astype(BF)
-        send_g[16 * q : 16 * q + 16, 2] = packed
+        send_m[16 * q : 16 * q + 16] = packed
+    loads[0].wait()
+    pack_channels(reader(g_ref), put_g)
 
     pl.semaphore_wait(barrier, TILES + 2)
+    exchange(send_m, got_m, 4)
     exchange(send_g, got_g, 0)
+    keep_own(send_m, got_m)
     keep_own(send_g, got_g)
-    loads[4].wait()
-    pack_channels(reader(x_ref), put_x)
-    keep_own(send_x, got_x)
 
     @pl.when(chip_y == FRAMES // 2 - 1)
     def _():
@@ -331,45 +335,62 @@
                 hop_copy(order, i).wait_send()
 
     row_refs = (row_grow, ends.at[0], row_centred, row_headed)
-    block_states(g_ref, c_rows, decays, False, row_refs, term.at[0], low.at[0])
+    block_scales(decays, False, shrink, row_grow, ends.at[0])
+    block_states(g_ref, c_rows, shrink, row_refs, term.at[0], low.at[0])
     for copy in swap_copies(0):
         copy.start()
-
-    wait_all(got_g, recv_sem.at[0])
-    exchange(send_x, got_x, 1, 0, EARLY)
-
-    def put_wide(q, k, value):
-        wide[16 * q : 16 * q + 16, pair(k)] = value.astype(BF)
-
-    unpack_channels(lambda q: got_g[8 * q : 8 * q + 8, 0:2], put_wide)
+    loads[4].wait()
+    pack_channels(reader(x_ref), put_x)
+    exchange(send_x, got_x, 1, 0, BEHIND)
+    keep_own(send_x, got_x)
+
+    wait_all(got_m, recv_sem.at[4])
     gather_maps = maps_matrix(3, 3, True)
     for q in range(4):
-        tiles = got_g[16 * q : 16 * q + 16, 2].astype(F32).reshape(TOKENS, LANES).astype(BF)
+        tiles = got_m[16 * q : 16 * q + 16].astype(F32).reshape(TOKENS, LANES).astype(BF)
         piece = nn(gather_maps, tiles).astype(BF)
         for p in range(3):
             col_maps[p, 32 * q : 32 * q + 32] = piece[32 * p : 32 * p + 32]
     col_refs = (col_grow, ends.at[1], col_centred, col_headed)
-    block_states(wide, col_maps[1], col_maps[2], True, col_refs, term.at[1], low.at[1])
+    block_scales(col_maps[2], True, shrink, col_grow, ends.at[1])
+    swapped(0)
+
+    wait_all(got_g, recv_sem.at[0])
+    exchange(send_x, got_x, 1, BEHIND, EARLY)
+
+    def put_wide(q, k, value):
+        wide[16 * q : 16 * q + 16, pair(k)] = value.astype(BF)
+
+    unpack_channels(lambda q: got_g[8 * q : 8 * q + 8], put_wide)
+    block_states(wide, col_maps[1], shrink, col_refs, term.at[1], low.at[1])
     for copy in swap_copies(1):
         copy.start()
-    filled = EARLY + PER_HOP * (FRAMES // 2 - 1 - chip_y)
+    filled = EARLY + PER_HOP * (FRAMES // 2 - chip_y)
+    exchange(send_x, got_x, 1, EARLY, filled)
     swapped(1)
-    exchange(send_x, got_x, 1, EARLY, filled)
     chain(1)
+
+    @pl.when(chip_y > 0)
+    def _():
+        chain(0)
+
     exchange(send_x, got_x, 1, filled)
     chain_end(1)
 
     def put_col(k, value):
         wide[:, pair(k)] = value.astype(BF)
 
-    grad_of_x(col_maps[0], col_maps[1], carry.at[1], True, col_refs, tails, put_col)
+    grad_of_x(col_maps[0], col_maps[1], lambda k: carry[1, k], True, col_refs, tails, put_col)
 
     def put_back(q, value):
         back_x[8 * q : 8 * q + 8] = value
 
     pack_channels(reader(wide), put_back)
-    swapped(0)
-    chain(0)
+
+    @pl.when(chip_y == 0)
+    def _():
+        chain(0)
+
     exchange(back_x, home_x, 2)
     keep_own(back_x, home_x)
 
@@ -392,7 +413,7 @@
         part_x[:, pair(k)] = value
 
     chain_end(0)
-    grad_of_x(b_rows, c_rows, carry.at[0], False, row_refs, tails, put_row)
+    grad_of_x(b_rows, c_rows, lambda k: carry[0, k], False, row_refs, tails, put_row)
     loads[5].wait()
     row_b, row_c = grads_of_maps(
         x_ref, b_rows, c_rows, saved_row, False, row_refs, tails, scaled)
@@ -416,10 +437,17 @@
 
     chain_sent(0)
     chain_sent(1)
+    wait_all(send_m, send_sem.at[4])
     wait_all(send_g, send_sem.at[0])
     wait_all(send_x, send_sem.at[1])
     wait_all(back_x, send_sem.at[2])
     wait_all(back_m, send_sem.at[3])
+
+
+def hand_over(x_in, b_in, c_in, x_out, b_out, c_out):
+    x_out[...] = x_in[...]
+    b_out[...] = b_in[...]
+    c_out[...] = c_in[...]
 
 
 def shards(inputs, grad_out, b_proj, c_proj, log_decay, saved_raster, saved_column):
@@ -441,14 +469,17 @@
             pltpu.VMEM((HEADS, TOKENS), BF),
             pltpu.VMEM((CHANNELS, STATE), F32),
             pltpu.VMEM((CHANNELS, STATE), F32),
-            pltpu.VMEM((TILES, 3, 8, LANES), BF),
+            pltpu.VMEM((TILES, 8, LANES), BF),
             pltpu.VMEM((TILES, 2, 8, LANES), BF),
-            pltpu.VMEM((TILES, 3, 8, LANES), BF),
+            pltpu.VMEM((TILES, 2, 8, LANES), BF),
+            pltpu.VMEM((TILES, 8, LANES), BF),
+            pltpu.VMEM((TILES, 2, 8, LANES), BF),
             pltpu.VMEM((TILES, 2, 8, LANES), BF),
             pltpu.VMEM((TILES, 2, 8, LANES), BF),
             pltpu.VMEM((TILES, 4, LANES), BF),
             pltpu.VMEM((TILES, 2, 8, LANES), BF),
             pltpu.VMEM((TILES, 4, LANES), BF),
+            pltpu.VMEM((TOKENS, CHANNELS), F32),
             pltpu.VMEM((TOKENS, CHANNELS), F32),
             pltpu.VMEM((TOKENS, CHANNELS), BF),
             pltpu.VMEM((TOKENS, CHANNELS), BF),
@@ -470,8 +501,8 @@
             pltpu.VMEM((3, TOKENS, LANES), BF),
             pltpu.VMEM((TOKENS, CHANNELS), F32),
             pltpu.SemaphoreType.DMA((7,)),
-            pltpu.SemaphoreType.DMA((4,)),
-            pltpu.SemaphoreType.DMA((4,)),
+            pltpu.SemaphoreType.DMA((5,)),
+            pltpu.SemaphoreType.DMA((5,)),
             pltpu.SemaphoreType.DMA((2, 2)),
             pltpu.SemaphoreType.DMA((2, 2)),
             pltpu.SemaphoreType.DMA((2, HALF)),
@@ -495,6 +526,19 @@
         saved_raster.reshape(CHANNELS, STATE),
         saved_column.reshape(CHANNELS, STATE),
     )
+    out_x, out_b, out_c = pl.pallas_call(
+        hand_over,
+        out_shape=(
+            jax.ShapeDtypeStruct((TOKENS, CHANNELS), BF),
+            jax.ShapeDtypeStruct((TOKENS, STATE), BF),
+            jax.ShapeDtypeStruct((TOKENS, STATE), BF),
+        ),
+        in_specs=[vmem] * 3,
+        out_specs=(vmem, vmem, vmem),
+        compiler_params=pltpu.CompilerParams(vmem_limit_bytes=63 * 1024 * 1024),
+        cost_estimate=pl.CostEstimate(flops=0, bytes_accessed=640_000, transcendentals=0),
+        name="hand_over",
+    )(out_x, out_b, out_c)
     return (
         out_x.reshape(1, 1, TOKENS, CHANNELS),
         out_b.reshape(1, 1, TOKENS, STATE),

time: 78.6 us -> 76.1 us (0.968)
  local copies, waits for them, and re-layouts: 3.06 us -> 0 us
    unnamed x7 -> x0, local copies, waits for them, and re-layouts: 3.06 us -> none
    pallas_call x0 -> x1, Pallas kernels: none -> 1.7 us  [shards(): pl.pallas_call(hand_over, out_shape=(jax.ShapeDtypeStruct((TOKENS, CHANNE...]
    pallas_call x1, Pallas kernels: 74.7 us -> 73.6 us  [shards(): pl.pallas_call(kernel, out_shape=(jax.ShapeDtypeStruct((TOKENS, CHANNELS)...]
where the time goes in v2:
time: 76.1 us; the launch traced here: 76 us
  Pallas kernels  75.3 us (99%)
    pallas_call x1, Pallas kernels, shards(): pl.pallas_call(kernel, out_shape=(jax.ShapeDtypeStruct((TOKENS, CHANNELS)...  73.6 us
    pallas_call x1, Pallas kernels, shards(): pl.pallas_call(hand_over, out_shape=(jax.ShapeDtypeStruct((TOKENS, CHANNE...  1.7 us

profile of v2, /device:TPU:1, one launch (start us, length us, event | category | flops | bytes accessed | tf_op | source)
XLA Modules:
  0.0 76.0 jit_solution(14261915601888158695)
XLA Ops:
  0.6 73.6 %scan_backward.1 = (bf16[128,1024]{1,0:T(8,128)(2,1)}, bf16[128,128]{1,0:T(8,128)(2,1)}, bf16[128,128]{1,0:T(8,128)(2,1)}) custom-call(bf16[128,1024]{1,0:T(8,128)(2,1)} %bitcast.12, bf16[128,1024]{1,0:T(8,128)(2,1)} %bitcast.13, bf16[128,128]{1,0:T(8,128)(2,1)} %bitcast.15, bf16[128,128]{1,0:T(8,128)(2,1)} %bitcast.16, bf16[16,128]{1,0:T(8,128)(2,1)} %bitcast.19, ...), custom_call_target="tpu_custom_call" | custom-call | flops 800000000 | bytes 2600000 | tf_op jit(solution)/shard_map/scan_backward/pallas_call | solution.py:455
  74.3 1.7 %hand_over.1 = (bf16[128,1024]{1,0:T(8,128)(2,1)}, bf16[128,128]{1,0:T(8,128)(2,1)}, bf16[128,128]{1,0:T(8,128)(2,1)}) custom-call(bf16[128,1024]{1,0:T(8,128)(2,1)} %get-tuple-element.9.x_in, bf16[128,128]{1,0:T(8,128)(2,1)} %get-tuple-element.10.b_in, bf16[128,128]{1,0:T(8,128)(2,1)} %get-tuple-element.11.c_in), custom_call_target="tpu_custom_call" | custom-call | bytes 640000 | tf_op jit(solution)/shard_map/hand_over/pallas_call | solution.py:529

commit v3 on v2

--- a/solution.py
+++ b/solution.py
@@ -18,8 +18,10 @@
 FRAMES = 8
 HALF = PAIRS // 2
 BEHIND = 8
-EARLY = 20
-PER_HOP = 7
+EARLY = 14
+PER_HOP = 4
+PIECES = (1, 2)
+PIECES_MAX = 2
 BF = jnp.bfloat16
 F32 = jnp.float32
 MESH = pl.DeviceIdType.MESH
@@ -121,15 +123,18 @@
         ends[k, 1:2, :] = jnp.exp(total)
 
 
-def block_states(grad, c_rows, shrink, refs, term, low):
+def scale_grad(value, rows, k, shrink, refs):
+    grow, ends, centred, headed = refs
+    shrunk = value.astype(F32) * shrink[rows, pair(k)]
+    centred[rows, pair(k)] = shrunk.astype(BF)
+    headed[rows, pair(k)] = (shrunk * ends[k, 0:1, :]).astype(BF)
+
+
+def block_states(c_rows, refs, term, low):
     grow, ends, centred, headed = refs
     c_turned = nt(identity(), c_rows).astype(BF)
     for k in range(PAIRS):
-        shrunk = grad[:, pair(k)].astype(F32) * shrink[:, pair(k)]
-        centred[:, pair(k)] = shrunk.astype(BF)
-        by_head = (shrunk * ends[k, 0:1, :]).astype(BF)
-        headed[:, pair(k)] = by_head
-        state = nn(c_turned, by_head)
+        state = nn(c_turned, headed[:, pair(k)])
         term[k] = state
         low[k] = state.astype(BF)
 
@@ -157,13 +162,14 @@
 
 def kernel(
     x_hbm, g_hbm, b_hbm, c_hbm, d_hbm, saved_row_hbm, saved_col_hbm,
+    out_x_hbm, out_b_hbm, out_c_hbm,
     out_x, out_b, out_c,
     x_ref, g_ref, b_ref, c_ref, d_ref, saved_row, saved_col,
     send_m, send_g, send_x, got_m, got_g, got_x, back_x, back_m, home_x, home_m,
     shrink, row_grow, row_centred, row_headed, col_grow, col_centred, col_headed,
     term, low, ends, peer_low, peer_ends, incoming, outgoing, give, carry,
     tails, scaled, wide, col_maps, part_x,
-    load_sem, send_sem, recv_sem, swap_send, swap_recv, hop_send, hop_recv, give_send, give_recv,
+    load_sem, store_sem, send_sem, recv_sem, swap_send, swap_recv, hop_send, hop_recv, give_send, give_recv,
 ):
     f = lax.axis_index("frames")
     me = lax.axis_index("tiles")
@@ -238,11 +244,10 @@
         stack = jnp.concatenate([b_rows[rows], c_rows[rows], decays[rows]], axis=0)
         packed = nn(spread_maps, stack).reshape(16, 8, LANES).astype(BF)
         send_m[16 * q : 16 * q + 16] = packed
+    pl.semaphore_wait(barrier, TILES + 2)
+    exchange(send_m, got_m, 4)
     loads[0].wait()
     pack_channels(reader(g_ref), put_g)
-
-    pl.semaphore_wait(barrier, TILES + 2)
-    exchange(send_m, got_m, 4)
     exchange(send_g, got_g, 0)
     keep_own(send_m, got_m)
     keep_own(send_g, got_g)
@@ -267,22 +272,26 @@
             ])
         ]
 
-    def hop_copy(order, i):
+    def rows_of(order, p):
+        rows = STATE // PIECES[order]
+        return pl.ds(rows * p, rows)
+
+    def hop_copy(order, i, p):
         return pltpu.make_async_remote_copy(
-            src_ref=outgoing.at[order, i],
-            dst_ref=incoming.at[order, i],
-            send_sem=hop_send.at[order, i],
-            recv_sem=hop_recv.at[order, i],
+            src_ref=outgoing.at[order, i, rows_of(order, p)],
+            dst_ref=incoming.at[order, i, rows_of(order, p)],
+            send_sem=hop_send.at[order, i, p],
+            recv_sem=hop_recv.at[order, i, p],
             device_id=(below, me),
             device_id_type=MESH,
         )
 
-    def give_copy(order, i):
+    def give_copy(order, i, p):
         return pltpu.make_async_remote_copy(
-            src_ref=give.at[order, i],
-            dst_ref=carry.at[order, mine + i],
-            send_sem=give_send.at[order, i],
-            recv_sem=give_recv.at[order, i],
+            src_ref=give.at[order, i, rows_of(order, p)],
+            dst_ref=carry.at[order, mine + i, rows_of(order, p)],
+            send_sem=give_send.at[order, i, p],
+            recv_sem=give_recv.at[order, i, p],
             device_id=(other, me),
             device_id_type=MESH,
         )
@@ -291,52 +300,56 @@
         for copy in swap_copies(order):
             copy.wait_recv()
 
+    def steps(order):
+        return [(i, p) for i in range(HALF) for p in range(PIECES[order])]
+
     def chain(order):
-        for i in range(HALF):
-            k = mine + i
-            own_state, peer_state = term[order, k], peer_low[order, i].astype(F32)
+        lower = core == 0
+        for i, p in steps(order):
+            k, rows = mine + i, rows_of(order, p)
+
+            @pl.when(chip_y < FRAMES // 2 - 1)
+            def _():
+                hop_copy(order, i, p).wait_recv()
+
+            own_state, peer_state = term[order, k, rows], peer_low[order, i, rows].astype(F32)
             own_decay, peer_decay = ends[order, k, 1:2, :], peer_ends[order, k, 1:2, :]
-            lower = core == 0
             lower_state = jnp.where(lower, own_state, peer_state)
             upper_state = jnp.where(lower, peer_state, own_state)
             lower_decay = jnp.where(lower, own_decay, peer_decay)
             upper_decay = jnp.where(lower, peer_decay, own_decay)
-
-            @pl.when(chip_y < FRAMES // 2 - 1)
-            def _():
-                hop_copy(order, i).wait_recv()
-
-            entering = incoming[order, i].astype(F32)
+            entering = incoming[order, i, rows].astype(F32)
             between = upper_decay * entering + upper_state
 
             @pl.when(chip_y > 0)
             def _():
-                outgoing[order, i] = (lower_decay * between + lower_state).astype(BF)
-                hop_copy(order, i).start()
-
-            carry[order, k] = jnp.where(lower, between, entering).astype(BF)
-            give[order, i] = jnp.where(lower, entering, between).astype(BF)
-            give_copy(order, i).start()
+                outgoing[order, i, rows] = (lower_decay * between + lower_state).astype(BF)
+                hop_copy(order, i, p).start()
+
+            carry[order, k, rows] = jnp.where(lower, between, entering).astype(BF)
+            give[order, i, rows] = jnp.where(lower, entering, between).astype(BF)
+            give_copy(order, i, p).start()
 
     def chain_end(order):
-        for i in range(HALF):
-            pltpu.make_async_copy(
-                carry.at[order, theirs + i], carry.at[order, theirs + i], give_recv.at[order, i]
-            ).wait()
+        for i, p in steps(order):
+            some = carry.at[order, theirs + i, rows_of(order, p)]
+            pltpu.make_async_copy(some, some, give_recv.at[order, i, p]).wait()
 
     def chain_sent(order):
         for copy in swap_copies(order):
             copy.wait_send()
-        for i in range(HALF):
-            give_copy(order, i).wait_send()
+        for i, p in steps(order):
+            give_copy(order, i, p).wait_send()
 
             @pl.when(chip_y > 0)
             def _():
-                hop_copy(order, i).wait_send()
+                hop_copy(order, i, p).wait_send()
 
     row_refs = (row_grow, ends.at[0], row_centred, row_headed)
     block_scales(decays, False, shrink, row_grow, ends.at[0])
-    block_states(g_ref, c_rows, shrink, row_refs, term.at[0], low.at[0])
+    for k in range(PAIRS):
+        scale_grad(g_ref[:, pair(k)], slice(0, TOKENS), k, shrink, row_refs)
+    block_states(c_rows, row_refs, term.at[0], low.at[0])
     for copy in swap_copies(0):
         copy.start()
     loads[4].wait()
@@ -361,8 +374,11 @@
     def put_wide(q, k, value):
         wide[16 * q : 16 * q + 16, pair(k)] = value.astype(BF)
 
-    unpack_channels(lambda q: got_g[8 * q : 8 * q + 8], put_wide)
-    block_states(wide, col_maps[1], shrink, col_refs, term.at[1], low.at[1])
+    def put_scaled(q, k, value):
+        scale_grad(value, slice(16 * q, 16 * q + 16), k, shrink, col_refs)
+
+    unpack_channels(lambda q: got_g[8 * q : 8 * q + 8], put_scaled)
+    block_states(col_maps[1], col_refs, term.at[1], low.at[1])
     for copy in swap_copies(1):
         copy.start()
     filled = EARLY + PER_HOP * (FRAMES // 2 - chip_y)
@@ -426,6 +442,13 @@
 
     unpack_channels(lambda q: home_x[8 * q : 8 * q + 8], put_sum)
 
+    stores = [
+        pltpu.make_async_copy(source, target, store_sem.at[i])
+        for i, (source, target) in enumerate(
+            [(out_x, out_x_hbm), (out_b, out_b_hbm), (out_c, out_c_hbm)])
+    ]
+    stores[0].start()
+
     wait_all(home_m, recv_sem.at[3])
     gather_back = maps_matrix(2, 2, True)
     for q in range(4):
@@ -435,6 +458,8 @@
         out_b[rows, :] = (row_b[rows] + both[0:32]).astype(BF)
         out_c[rows, :] = (row_c[rows] + both[32:64]).astype(BF)
 
+    stores[1].start()
+    stores[2].start()
     chain_sent(0)
     chain_sent(1)
     wait_all(send_m, send_sem.at[4])
@@ -442,16 +467,25 @@
     wait_all(send_x, send_sem.at[1])
     wait_all(back_x, send_sem.at[2])
     wait_all(back_m, send_sem.at[3])
-
-
-def hand_over(x_in, b_in, c_in, x_out, b_out, c_out):
-    x_out[...] = x_in[...]
-    b_out[...] = b_in[...]
-    c_out[...] = c_in[...]
+    for store in stores:
+        store.wait()
+
+
+def hand_over(x_in, b_in, c_in, x_out, b_out, c_out, x_held, b_held, c_held, load_sem, store_sem):
+    parts = [(x_in, x_held, x_out), (b_in, b_held, b_out), (c_in, c_held, c_out)]
+    loads = [pltpu.make_async_copy(p[0], p[1], load_sem.at[i]) for i, p in enumerate(parts)]
+    stores = [pltpu.make_async_copy(p[1], p[2], store_sem.at[i]) for i, p in enumerate(parts)]
+    for load in loads:
+        load.start()
+    for load, store in zip(loads, stores):
+        load.wait()
+        store.start()
+    for store in stores:
+        store.wait()
 
 
 def shards(inputs, grad_out, b_proj, c_proj, log_decay, saved_raster, saved_column):
-    vmem = pl.BlockSpec(memory_space=pltpu.VMEM)
+    anywhere = pl.BlockSpec(memory_space=pl.ANY)
     out_x, out_b, out_c = pl.pallas_call(
         kernel,
         out_shape=(
@@ -460,8 +494,11 @@
             jax.ShapeDtypeStruct((TOKENS, STATE), BF),
         ),
         in_specs=[pl.BlockSpec(memory_space=pltpu.HBM)] * 7,
-        out_specs=(vmem, vmem, vmem),
+        out_specs=(anywhere, anywhere, anywhere),
         scratch_shapes=[
+            pltpu.VMEM((TOKENS, CHANNELS), BF),
+            pltpu.VMEM((TOKENS, STATE), BF),
+            pltpu.VMEM((TOKENS, STATE), BF),
             pltpu.VMEM((TOKENS, CHANNELS), BF),
             pltpu.VMEM((TOKENS, CHANNELS), BF),
             pltpu.VMEM((TOKENS, STATE), BF),
@@ -501,14 +538,15 @@
             pltpu.VMEM((3, TOKENS, LANES), BF),
             pltpu.VMEM((TOKENS, CHANNELS), F32),
             pltpu.SemaphoreType.DMA((7,)),
+            pltpu.SemaphoreType.DMA((3,)),
             pltpu.SemaphoreType.DMA((5,)),
             pltpu.SemaphoreType.DMA((5,)),
             pltpu.SemaphoreType.DMA((2, 2)),
             pltpu.SemaphoreType.DMA((2, 2)),
-            pltpu.SemaphoreType.DMA((2, HALF)),
-            pltpu.SemaphoreType.DMA((2, HALF)),
-            pltpu.SemaphoreType.DMA((2, HALF)),
-            pltpu.SemaphoreType.DMA((2, HALF)),
+            pltpu.SemaphoreType.DMA((2, HALF, PIECES_MAX)),
+            pltpu.SemaphoreType.DMA((2, HALF, PIECES_MAX)),
+            pltpu.SemaphoreType.DMA((2, HALF, PIECES_MAX)),
+            pltpu.SemaphoreType.DMA((2, HALF, PIECES_MAX)),
         ],
         compiler_params=pltpu.CompilerParams(
             collective_id=0, has_side_effects=True, vmem_limit_bytes=63 * 1024 * 1024
@@ -533,8 +571,15 @@
             jax.ShapeDtypeStruct((TOKENS, STATE), BF),
             jax.ShapeDtypeStruct((TOKENS, STATE), BF),
         ),
-        in_specs=[vmem] * 3,
-        out_specs=(vmem, vmem, vmem),
+        in_specs=[anywhere] * 3,
+        out_specs=(anywhere, anywhere, anywhere),
+        scratch_shapes=[
+            pltpu.VMEM((TOKENS, CHANNELS), BF),
+            pltpu.VMEM((TOKENS, STATE), BF),
+            pltpu.VMEM((TOKENS, STATE), BF),
+            pltpu.SemaphoreType.DMA((3,)),
+            pltpu.SemaphoreType.DMA((3,)),
+        ],
         compiler_params=pltpu.CompilerParams(vmem_limit_bytes=63 * 1024 * 1024),
         cost_estimate=pl.CostEstimate(flops=0, bytes_accessed=640_000, transcendentals=0),
         name="hand_over",

time: 76.1 us -> 76.8 us (level)
  no operation moved by 1% of the time
where the time goes in v3:
time: 76.8 us; the launch traced here: 76.5 us
  Pallas kernels  75.8 us (99%)
    pallas_call x1, Pallas kernels, shards(): pl.pallas_call(kernel, out_shape=(jax.ShapeDtypeStruct((TOKENS, CHANNELS)...  74.1 us
    pallas_call x1, Pallas kernels, shards(): pl.pallas_call(hand_over, out_shape=(jax.ShapeDtypeStruct((TOKENS, CHANNE...  1.71 us

profile of v3, /device:TPU:1, one launch (start us, length us, event | category | flops | bytes accessed | tf_op | source)
XLA Modules:
  0.0 76.5 jit_solution(11542298888498813970)
XLA Ops:
  0.6 74.1 %scan_backward.1 = (bf16[128,1024]{1,0:T(8,128)(2,1)}, bf16[128,128]{1,0:T(8,128)(2,1)}, bf16[128,128]{1,0:T(8,128)(2,1)}) custom-call(bf16[128,1024]{1,0:T(8,128)(2,1)} %bitcast.12, bf16[128,1024]{1,0:T(8,128)(2,1)} %bitcast.13, bf16[128,128]{1,0:T(8,128)(2,1)} %bitcast.15, bf16[128,128]{1,0:T(8,128)(2,1)} %bitcast.16, bf16[16,128]{1,0:T(8,128)(2,1)} %bitcast.19, ...), custom_call_target="tpu_custom_call" | custom-call | flops 800000000 | bytes 2600000 | tf_op jit(solution)/shard_map/scan_backward/pallas_call | solution.py:489
  74.8 1.7 %hand_over.1 = (bf16[128,1024]{1,0:T(8,128)(2,1)}, bf16[128,128]{1,0:T(8,128)(2,1)}, bf16[128,128]{1,0:T(8,128)(2,1)}) custom-call(bf16[128,1024]{1,0:T(8,128)(2,1)} %get-tuple-element.9.x_in, bf16[128,128]{1,0:T(8,128)(2,1)} %get-tuple-element.10.b_in, bf16[128,128]{1,0:T(8,128)(2,1)} %get-tuple-element.11.c_in), custom_call_target="tpu_custom_call" | custom-call | bytes 640000 | tf_op jit(solution)/shard_map/hand_over/pallas_call | solution.py:567

commit v4 on v3

--- a/solution.py
+++ b/solution.py
@@ -20,6 +20,7 @@
 BEHIND = 8
 EARLY = 14
 PER_HOP = 4
+MEANWHILE = 12
 PIECES = (1, 2)
 PIECES_MAX = 2
 BF = jnp.bfloat16
@@ -385,12 +386,7 @@
     exchange(send_x, got_x, 1, EARLY, filled)
     swapped(1)
     chain(1)
-
-    @pl.when(chip_y > 0)
-    def _():
-        chain(0)
-
-    exchange(send_x, got_x, 1, filled)
+    exchange(send_x, got_x, 1, filled, filled + MEANWHILE)
     chain_end(1)
 
     def put_col(k, value):
@@ -402,11 +398,8 @@
         back_x[8 * q : 8 * q + 8] = value
 
     pack_channels(reader(wide), put_back)
-
-    @pl.when(chip_y == 0)
-    def _():
-        chain(0)
-
+    chain(0)
+    exchange(send_x, got_x, 1, filled + MEANWHILE)
     exchange(back_x, home_x, 2)
     keep_own(back_x, home_x)
 

time: 76.8 us -> 77.3 us (level)
  no operation moved by 1% of the time
where the time goes in v4:
time: 77.3 us; the launch traced here: 77.2 us
  Pallas kernels  76.5 us (99%)
    pallas_call x1, Pallas kernels, shards(): pl.pallas_call(kernel, out_shape=(jax.ShapeDtypeStruct((TOKENS, CHANNELS)...  74.8 us
    pallas_call x1, Pallas kernels, shards(): pl.pallas_call(hand_over, out_shape=(jax.ShapeDtypeStruct((TOKENS, CHANNE...  1.71 us

profile of v4, /device:TPU:1, one launch (start us, length us, event | category | flops | bytes accessed | tf_op | source)
XLA Modules:
  0.0 77.2 jit_solution(15722747924635617940)
XLA Ops:
  0.6 74.8 %scan_backward.1 = (bf16[128,1024]{1,0:T(8,128)(2,1)}, bf16[128,128]{1,0:T(8,128)(2,1)}, bf16[128,128]{1,0:T(8,128)(2,1)}) custom-call(bf16[128,1024]{1,0:T(8,128)(2,1)} %bitcast.12, bf16[128,1024]{1,0:T(8,128)(2,1)} %bitcast.13, bf16[128,128]{1,0:T(8,128)(2,1)} %bitcast.15, bf16[128,128]{1,0:T(8,128)(2,1)} %bitcast.16, bf16[16,128]{1,0:T(8,128)(2,1)} %bitcast.19, ...), custom_call_target="tpu_custom_call" | custom-call | flops 800000000 | bytes 2600000 | tf_op jit(solution)/shard_map/scan_backward/pallas_call | solution.py:482
  75.5 1.7 %hand_over.1 = (bf16[128,1024]{1,0:T(8,128)(2,1)}, bf16[128,128]{1,0:T(8,128)(2,1)}, bf16[128,128]{1,0:T(8,128)(2,1)}) custom-call(bf16[128,1024]{1,0:T(8,128)(2,1)} %get-tuple-element.9.x_in, bf16[128,128]{1,0:T(8,128)(2,1)} %get-tuple-element.10.b_in, bf16[128,128]{1,0:T(8,128)(2,1)} %get-tuple-element.11.c_in), custom_call_target="tpu_custom_call" | custom-call | bytes 640000 | tf_op jit(solution)/shard_map/hand_over/pallas_call | solution.py:560

commit v5 on v4

--- a/solution.py
+++ b/solution.py
@@ -18,9 +18,9 @@
 FRAMES = 8
 HALF = PAIRS // 2
 BEHIND = 8
-EARLY = 14
-PER_HOP = 4
-MEANWHILE = 12
+EARLY = 20
+PER_HOP = 7
+LEFT = 6
 PIECES = (1, 2)
 PIECES_MAX = 2
 BF = jnp.bfloat16
@@ -187,9 +187,11 @@
         load.start()
 
     def partner(k):
-        step = TILES - 1 - k
-        u, dx = lax.div(step, DEPTH_X), lax.rem(step, DEPTH_X)
-        dz = lax.div(u + 1, 2) * (2 * lax.rem(u, 2) - 1)
+        step = TILES + 3 - k
+        far, r = lax.div(step, 8), lax.rem(step, 8)
+        most, none = lax.div(far, 8), lax.div(8 - far, 8)
+        dx = (1 - most - none) * lax.div(r, 2) + most * r + none * (r - DEPTH_X)
+        dz = far * (1 - 2 * lax.rem(r, 2))
         return lax.rem(z + dz + DEPTH_Z, DEPTH_Z) * DEPTH_X + lax.rem(x + dx, DEPTH_X)
 
     barrier = pltpu.get_barrier_semaphore()
@@ -382,11 +384,12 @@
     block_states(col_maps[1], col_refs, term.at[1], low.at[1])
     for copy in swap_copies(1):
         copy.start()
-    filled = EARLY + PER_HOP * (FRAMES // 2 - chip_y)
+    filled = EARLY + 3 + PER_HOP * (FRAMES // 2 - 1 - chip_y)
+    packed_by = TILES - 1 - LEFT * chip_y
     exchange(send_x, got_x, 1, EARLY, filled)
     swapped(1)
     chain(1)
-    exchange(send_x, got_x, 1, filled, filled + MEANWHILE)
+    exchange(send_x, got_x, 1, filled, packed_by)
     chain_end(1)
 
     def put_col(k, value):
@@ -399,7 +402,7 @@
 
     pack_channels(reader(wide), put_back)
     chain(0)
-    exchange(send_x, got_x, 1, filled + MEANWHILE)
+    exchange(send_x, got_x, 1, packed_by)
     exchange(back_x, home_x, 2)
     keep_own(back_x, home_x)
 

time: 77.3 us -> 76 us (0.983)
  Pallas kernels: 76.5 us -> 75.1 us
    pallas_call x1, Pallas kernels: 74.8 us -> 73.4 us  [shards(): pl.pallas_call(kernel, out_shape=(jax.ShapeDtypeStruct((TOKENS, CHANNELS)...]
where the time goes in v5:
time: 76 us; the launch traced here: 75.8 us
  Pallas kernels  75.1 us (99%)
    pallas_call x1, Pallas kernels, shards(): pl.pallas_call(kernel, out_shape=(jax.ShapeDtypeStruct((TOKENS, CHANNELS)...  73.4 us
    pallas_call x1, Pallas kernels, shards(): pl.pallas_call(hand_over, out_shape=(jax.ShapeDtypeStruct((TOKENS, CHANNE...  1.71 us

profile of v5, /device:TPU:1, one launch (start us, length us, event | category | flops | bytes accessed | tf_op | source)
XLA Modules:
  0.0 75.8 jit_solution(1880150047847372838)
XLA Ops:
  0.6 73.4 %scan_backward.1 = (bf16[128,1024]{1,0:T(8,128)(2,1)}, bf16[128,128]{1,0:T(8,128)(2,1)}, bf16[128,128]{1,0:T(8,128)(2,1)}) custom-call(bf16[128,1024]{1,0:T(8,128)(2,1)} %bitcast.12, bf16[128,1024]{1,0:T(8,128)(2,1)} %bitcast.13, bf16[128,128]{1,0:T(8,128)(2,1)} %bitcast.15, bf16[128,128]{1,0:T(8,128)(2,1)} %bitcast.16, bf16[16,128]{1,0:T(8,128)(2,1)} %bitcast.19, ...), custom_call_target="tpu_custom_call" | custom-call | flops 800000000 | bytes 2600000 | tf_op jit(solution)/shard_map/scan_backward/pallas_call | solution.py:485
  74.1 1.7 %hand_over.1 = (bf16[128,1024]{1,0:T(8,128)(2,1)}, bf16[128,128]{1,0:T(8,128)(2,1)}, bf16[128,128]{1,0:T(8,128)(2,1)}) custom-call(bf16[128,1024]{1,0:T(8,128)(2,1)} %get-tuple-element.9.x_in, bf16[128,128]{1,0:T(8,128)(2,1)} %get-tuple-element.10.b_in, bf16[128,128]{1,0:T(8,128)(2,1)} %get-tuple-element.11.c_in), custom_call_target="tpu_custom_call" | custom-call | bytes 640000 | tf_op jit(solution)/shard_map/hand_over/pallas_call | solution.py:563

commit v6 on v5

--- a/solution.py
+++ b/solution.py
@@ -17,7 +17,7 @@
 DEPTH_X = 4
 FRAMES = 8
 HALF = PAIRS // 2
-BEHIND = 8
+BEHIND = 20
 EARLY = 20
 PER_HOP = 7
 LEFT = 6
@@ -80,14 +80,14 @@
     return ones_where(r == c)
 
 
-def maps_matrix(bits, parts, back=False):
-    shape = (16 << bits, 32 * parts)
+def maps_matrix(parts, back=False):
+    shape = (32 * parts, 32 * parts)
     if back:
         c, r = square(shape[::-1])
     else:
         r, c = square(shape)
     part, token = high(c, 5), c & 31
-    return ones_where(r == lax.shift_left(high(token, 1), bits) + part * 2 + (token & 1))
+    return ones_where(r == high(token, 1) * (2 * parts) + part * 2 + (token & 1))
 
 
 def pair(k):
@@ -183,8 +183,27 @@
             (saved_row_hbm, saved_row), (saved_col_hbm, saved_col),
         ])
     ]
-    for load in loads:
+    for load in loads[:4]:
         load.start()
+
+    xs = [lax.rem(x + dx, DEPTH_X) for dx in range(DEPTH_X)]
+
+    def each_partner(act):
+        opposite = lax.rem(z + DEPTH_Z // 2, DEPTH_Z) * DEPTH_X
+        for dx in range(DEPTH_X):
+            act(opposite + xs[dx])
+
+        @pl.loop(1, DEPTH_Z // 2)
+        def _(k):
+            far = DEPTH_Z // 2 - k
+            ahead = lax.rem(z + far, DEPTH_Z) * DEPTH_X
+            behind = lax.rem(z - far + DEPTH_Z, DEPTH_Z) * DEPTH_X
+            for dx in range(DEPTH_X):
+                act(ahead + xs[dx])
+                act(behind + xs[dx])
+
+        for dx in range(1, DEPTH_X):
+            act(z * DEPTH_X + xs[dx])
 
     def partner(k):
         step = TILES + 3 - k
@@ -196,9 +215,10 @@
 
     barrier = pltpu.get_barrier_semaphore()
 
-    @pl.loop(0, TILES - 1)
-    def _(k):
-        pl.semaphore_signal(barrier, inc=1, device_id=(f, partner(k)), device_id_type=MESH)
+    def greet(peer):
+        pl.semaphore_signal(barrier, inc=1, device_id=(f, peer), device_id_type=MESH)
+
+    each_partner(greet)
 
     core, chip_y = lax.rem(f, 2), lax.div(f, 2)
     other = f + 1 - 2 * core
@@ -207,21 +227,29 @@
     for neighbour in (other, above, below):
         pl.semaphore_signal(barrier, inc=1, device_id=(neighbour, me), device_id_type=MESH)
 
+    for load in loads[4:]:
+        load.start()
+
     def keep_own(source, target):
         target[pl.ds(me, 1)] = source[pl.ds(me, 1)]
 
-    def exchange(source, target, which, first=0, last=TILES - 1):
+    def send(source, target, which, peer):
+        pltpu.make_async_remote_copy(
+            src_ref=source.at[peer],
+            dst_ref=target.at[me],
+            send_sem=send_sem.at[which],
+            recv_sem=recv_sem.at[which],
+            device_id=(f, peer),
+            device_id_type=MESH,
+        ).start()
+
+    def exchange(source, target, which):
+        each_partner(lambda peer: send(source, target, which, peer))
+
+    def exchange_some(source, target, which, first, last=TILES - 1):
         @pl.loop(first, last)
         def _(k):
-            peer = partner(k)
-            pltpu.make_async_remote_copy(
-                src_ref=source.at[peer],
-                dst_ref=target.at[me],
-                send_sem=send_sem.at[which],
-                recv_sem=recv_sem.at[which],
-                device_id=(f, peer),
-                device_id_type=MESH,
-            ).start()
+            send(source, target, which, partner(k))
 
     def wait_all(ref, sem):
         some = ref.at[pl.ds(0, TILES - 1)]
@@ -241,11 +269,11 @@
     decays = nt(identity(), jnp.concatenate(
         [d_ref[...], jnp.zeros((TOKENS - HEADS, TOKENS), BF)], axis=0)).astype(BF)
     b_rows, c_rows = b_ref[...], c_ref[...]
-    spread_maps = maps_matrix(3, 3)
+    spread_maps = maps_matrix(3)
     for q in range(4):
         rows = slice(32 * q, 32 * q + 32)
         stack = jnp.concatenate([b_rows[rows], c_rows[rows], decays[rows]], axis=0)
-        packed = nn(spread_maps, stack).reshape(16, 8, LANES).astype(BF)
+        packed = nn(spread_maps, stack).reshape(16, 3, 2, LANES).astype(BF)
         send_m[16 * q : 16 * q + 16] = packed
     pl.semaphore_wait(barrier, TILES + 2)
     exchange(send_m, got_m, 4)
@@ -357,13 +385,13 @@
         copy.start()
     loads[4].wait()
     pack_channels(reader(x_ref), put_x)
-    exchange(send_x, got_x, 1, 0, BEHIND)
+    exchange_some(send_x, got_x, 1, 0, BEHIND)
     keep_own(send_x, got_x)
 
     wait_all(got_m, recv_sem.at[4])
-    gather_maps = maps_matrix(3, 3, True)
+    gather_maps = maps_matrix(3, True)
     for q in range(4):
-        tiles = got_m[16 * q : 16 * q + 16].astype(F32).reshape(TOKENS, LANES).astype(BF)
+        tiles = got_m[16 * q : 16 * q + 16].astype(F32).reshape(96, LANES).astype(BF)
         piece = nn(gather_maps, tiles).astype(BF)
         for p in range(3):
             col_maps[p, 32 * q : 32 * q + 32] = piece[32 * p : 32 * p + 32]
@@ -372,7 +400,6 @@
     swapped(0)
 
     wait_all(got_g, recv_sem.at[0])
-    exchange(send_x, got_x, 1, BEHIND, EARLY)
 
     def put_wide(q, k, value):
         wide[16 * q : 16 * q + 16, pair(k)] = value.astype(BF)
@@ -386,10 +413,10 @@
         copy.start()
     filled = EARLY + 3 + PER_HOP * (FRAMES // 2 - 1 - chip_y)
     packed_by = TILES - 1 - LEFT * chip_y
-    exchange(send_x, got_x, 1, EARLY, filled)
+    exchange_some(send_x, got_x, 1, EARLY, filled)
     swapped(1)
     chain(1)
-    exchange(send_x, got_x, 1, filled, packed_by)
+    exchange_some(send_x, got_x, 1, filled, packed_by)
     chain_end(1)
 
     def put_col(k, value):
@@ -402,7 +429,7 @@
 
     pack_channels(reader(wide), put_back)
     chain(0)
-    exchange(send_x, got_x, 1, packed_by)
+    exchange_some(send_x, got_x, 1, packed_by)
     exchange(back_x, home_x, 2)
     keep_own(back_x, home_x)
 
@@ -412,7 +439,7 @@
     col_b, col_c = grads_of_maps(
         wide, col_maps[0], col_maps[1], saved_col, True, col_refs, tails, scaled)
     col_b, col_c = col_b.astype(BF), col_c.astype(BF)
-    spread_back = maps_matrix(2, 2)
+    spread_back = maps_matrix(2)
     for q in range(4):
         rows = slice(32 * q, 32 * q + 32)
         stack = jnp.concatenate([col_b[rows], col_c[rows]], axis=0)
@@ -446,7 +473,7 @@
     stores[0].start()
 
     wait_all(home_m, recv_sem.at[3])
-    gather_back = maps_matrix(2, 2, True)
+    gather_back = maps_matrix(2, True)
     for q in range(4):
         rows = slice(32 * q, 32 * q + 32)
         tiles = home_m[16 * q : 16 * q + 16].astype(F32).reshape(64, LANES).astype(BF)
@@ -502,10 +529,10 @@
             pltpu.VMEM((HEADS, TOKENS), BF),
             pltpu.VMEM((CHANNELS, STATE), F32),
             pltpu.VMEM((CHANNELS, STATE), F32),
-            pltpu.VMEM((TILES, 8, LANES), BF),
+            pltpu.VMEM((TILES, 3, 2, LANES), BF),
             pltpu.VMEM((TILES, 2, 8, LANES), BF),
             pltpu.VMEM((TILES, 2, 8, LANES), BF),
-            pltpu.VMEM((TILES, 8, LANES), BF),
+            pltpu.VMEM((TILES, 3, 2, LANES), BF),
             pltpu.VMEM((TILES, 2, 8, LANES), BF),
             pltpu.VMEM((TILES, 2, 8, LANES), BF),
             pltpu.VMEM((TILES, 2, 8, LANES), BF),

time: 76 us -> 76.5 us (level)
  no operation moved by 1% of the time
where the time goes in v6:
time: 76.5 us; the launch traced here: 76.3 us
  Pallas kernels  75.7 us (99%)
    pallas_call x1, Pallas kernels, shards(): pl.pallas_call(kernel, out_shape=(jax.ShapeDtypeStruct((TOKENS, CHANNELS)...  73.9 us
    pallas_call x1, Pallas kernels, shards(): pl.pallas_call(hand_over, out_shape=(jax.ShapeDtypeStruct((TOKENS, CHANNE...  1.71 us

profile of v6, /device:TPU:1, one launch (start us, length us, event | category | flops | bytes accessed | tf_op | source)
XLA Modules:
  0.0 76.3 jit_solution(12022913311802020916)
XLA Ops:
  0.6 73.9 %scan_backward.1 = (bf16[128,1024]{1,0:T(8,128)(2,1)}, bf16[128,128]{1,0:T(8,128)(2,1)}, bf16[128,128]{1,0:T(8,128)(2,1)}) custom-call(bf16[128,1024]{1,0:T(8,128)(2,1)} %bitcast.12, bf16[128,1024]{1,0:T(8,128)(2,1)} %bitcast.13, bf16[128,128]{1,0:T(8,128)(2,1)} %bitcast.15, bf16[128,128]{1,0:T(8,128)(2,1)} %bitcast.16, bf16[16,128]{1,0:T(8,128)(2,1)} %bitcast.19, ...), custom_call_target="tpu_custom_call" | custom-call | flops 800000000 | bytes 2600000 | tf_op jit(solution)/shard_map/scan_backward/pallas_call | solution.py:512
  74.6 1.7 %hand_over.1 = (bf16[128,1024]{1,0:T(8,128)(2,1)}, bf16[128,128]{1,0:T(8,128)(2,1)}, bf16[128,128]{1,0:T(8,128)(2,1)}) custom-call(bf16[128,1024]{1,0:T(8,128)(2,1)} %get-tuple-element.9.x_in, bf16[128,128]{1,0:T(8,128)(2,1)} %get-tuple-element.10.b_in, bf16[128,128]{1,0:T(8,128)(2,1)} %get-tuple-element.11.c_in), custom_call_target="tpu_custom_call" | custom-call | bytes 640000 | tf_op jit(solution)/shard_map/hand_over/pallas_call | solution.py:590

commit v7 on v6

--- a/solution.py
+++ b/solution.py
@@ -17,8 +17,7 @@
 DEPTH_X = 4
 FRAMES = 8
 HALF = PAIRS // 2
-BEHIND = 20
-EARLY = 20
+BEHIND = 8
 PER_HOP = 7
 LEFT = 6
 PIECES = (1, 2)
@@ -411,9 +410,9 @@
     block_states(col_maps[1], col_refs, term.at[1], low.at[1])
     for copy in swap_copies(1):
         copy.start()
-    filled = EARLY + 3 + PER_HOP * (FRAMES // 2 - 1 - chip_y)
+    filled = BEHIND + PER_HOP * (FRAMES // 2 - chip_y)
     packed_by = TILES - 1 - LEFT * chip_y
-    exchange_some(send_x, got_x, 1, EARLY, filled)
+    exchange_some(send_x, got_x, 1, BEHIND, filled)
     swapped(1)
     chain(1)
     exchange_some(send_x, got_x, 1, filled, packed_by)

time: 76.5 us -> 75.6 us (0.988)
  Pallas kernels: 75.7 us -> 74.6 us
    pallas_call x1, Pallas kernels: 73.9 us -> 72.9 us  [shards(): pl.pallas_call(kernel, out_shape=(jax.ShapeDtypeStruct((TOKENS, CHANNELS)...]
where the time goes in v7:
time: 75.6 us; the launch traced here: 75.2 us
  Pallas kernels  74.6 us (99%)
    pallas_call x1, Pallas kernels, shards(): pl.pallas_call(kernel, out_shape=(jax.ShapeDtypeStruct((TOKENS, CHANNELS)...  72.9 us
    pallas_call x1, Pallas kernels, shards(): pl.pallas_call(hand_over, out_shape=(jax.ShapeDtypeStruct((TOKENS, CHANNE...  1.71 us

profile of v7, /device:TPU:1, one launch (start us, length us, event | category | flops | bytes accessed | tf_op | source)
XLA Modules:
  0.0 75.2 jit_solution(15962216174086886076)
XLA Ops:
  0.6 72.9 %scan_backward.1 = (bf16[128,1024]{1,0:T(8,128)(2,1)}, bf16[128,128]{1,0:T(8,128)(2,1)}, bf16[128,128]{1,0:T(8,128)(2,1)}) custom-call(bf16[128,1024]{1,0:T(8,128)(2,1)} %bitcast.12, bf16[128,1024]{1,0:T(8,128)(2,1)} %bitcast.13, bf16[128,128]{1,0:T(8,128)(2,1)} %bitcast.15, bf16[128,128]{1,0:T(8,128)(2,1)} %bitcast.16, bf16[16,128]{1,0:T(8,128)(2,1)} %bitcast.19, ...), custom_call_target="tpu_custom_call" | custom-call | flops 800000000 | bytes 2600000 | tf_op jit(solution)/shard_map/scan_backward/pallas_call | solution.py:511
  73.5 1.7 %hand_over.1 = (bf16[128,1024]{1,0:T(8,128)(2,1)}, bf16[128,128]{1,0:T(8,128)(2,1)}, bf16[128,128]{1,0:T(8,128)(2,1)}) custom-call(bf16[128,1024]{1,0:T(8,128)(2,1)} %get-tuple-element.9.x_in, bf16[128,128]{1,0:T(8,128)(2,1)} %get-tuple-element.10.b_in, bf16[128,128]{1,0:T(8,128)(2,1)} %get-tuple-element.11.c_in), custom_call_target="tpu_custom_call" | custom-call | bytes 640000 | tf_op jit(solution)/shard_map/hand_over/pallas_call | solution.py:589

commit v8 on v7

--- a/solution.py
+++ b/solution.py
@@ -20,6 +20,7 @@
 BEHIND = 8
 PER_HOP = 7
 LEFT = 6
+RETURNED = 20
 PIECES = (1, 2)
 PIECES_MAX = 2
 BF = jnp.bfloat16
@@ -427,9 +428,19 @@
         back_x[8 * q : 8 * q + 8] = value
 
     pack_channels(reader(wide), put_back)
-    chain(0)
+
+    @pl.when(chip_y > 0)
+    def _():
+        chain(0)
+
     exchange_some(send_x, got_x, 1, packed_by)
-    exchange(back_x, home_x, 2)
+    exchange_some(back_x, home_x, 2, 0, RETURNED)
+
+    @pl.when(chip_y == 0)
+    def _():
+        chain(0)
+
+    exchange_some(back_x, home_x, 2, RETURNED)
     keep_own(back_x, home_x)
 
     wait_all(got_x, recv_sem.at[1])

time: 75.6 us -> 74.5 us (0.985)
  Pallas kernels: 74.6 us -> 73.8 us
    pallas_call x1, Pallas kernels: 72.9 us -> 72 us  [shards(): pl.pallas_call(kernel, out_shape=(jax.ShapeDtypeStruct((TOKENS, CHANNELS)...]
where the time goes in v8:
time: 74.5 us; the launch traced here: 74.4 us
  Pallas kernels  73.8 us (99%)
    pallas_call x1, Pallas kernels, shards(): pl.pallas_call(kernel, out_shape=(jax.ShapeDtypeStruct((TOKENS, CHANNELS)...  72 us
    pallas_call x1, Pallas kernels, shards(): pl.pallas_call(hand_over, out_shape=(jax.ShapeDtypeStruct((TOKENS, CHANNE...  1.71 us

profile of v8, /device:TPU:1, one launch (start us, length us, event | category | flops | bytes accessed | tf_op | source)
XLA Modules:
  0.0 74.4 jit_solution(2378257484541771189)
XLA Ops:
  0.6 72.0 %scan_backward.1 = (bf16[128,1024]{1,0:T(8,128)(2,1)}, bf16[128,128]{1,0:T(8,128)(2,1)}, bf16[128,128]{1,0:T(8,128)(2,1)}) custom-call(bf16[128,1024]{1,0:T(8,128)(2,1)} %bitcast.12, bf16[128,1024]{1,0:T(8,128)(2,1)} %bitcast.13, bf16[128,128]{1,0:T(8,128)(2,1)} %bitcast.15, bf16[128,128]{1,0:T(8,128)(2,1)} %bitcast.16, bf16[16,128]{1,0:T(8,128)(2,1)} %bitcast.19, ...), custom_call_target="tpu_custom_call" | custom-call | flops 800000000 | bytes 2600000 | tf_op jit(solution)/shard_map/scan_backward/pallas_call | solution.py:522
  72.7 1.7 %hand_over.1 = (bf16[128,1024]{1,0:T(8,128)(2,1)}, bf16[128,128]{1,0:T(8,128)(2,1)}, bf16[128,128]{1,0:T(8,128)(2,1)}) custom-call(bf16[128,1024]{1,0:T(8,128)(2,1)} %get-tuple-element.9.x_in, bf16[128,128]{1,0:T(8,128)(2,1)} %get-tuple-element.10.b_in, bf16[128,128]{1,0:T(8,128)(2,1)} %get-tuple-element.11.c_in), custom_call_target="tpu_custom_call" | custom-call | bytes 640000 | tf_op jit(solution)/shard_map/hand_over/pallas_call | solution.py:600
